TPU v7x, 32 devices: a whole 2x2x4 slice. The times are simulated.
32 devices in a mesh: seq: 16 (over z, x, core), dp: 2 (over y).
Axes of the slice: x: 2, y: 2, z: 4, core: 2. Of those that a mesh axis runs over, the one named last changes fastest.
Arguments:
- inputs: bfloat16 [2, 2048, 768], P('dp', 'seq'), may hold values from -150 to 150
- cotangent: bfloat16 [2, 2048, 768], P('dp', 'seq'), may hold values from -6 to 6
- conv_weight: bfloat16 [768, 768], replicated, may hold values from -0.125 to 0.125
- proj_weight: bfloat16 [256, 768], replicated, may hold values from -0.375 to 0.375
- gain_in: float32 [768], replicated, may hold values from 0.5 to 1.5
- bias_in: float32 [768], replicated, may hold values from -0.5 to 0.5
- gain_mid: float32 [256], replicated, may hold values from 0.5 to 1.5
- bias_mid: float32 [256], replicated, may hold values from -0.5 to 0.5
Outputs:
- block_out: bfloat16 [2, 2048, 768], P('dp', 'seq')
- input_grad: bfloat16 [2, 2048, 768], P('dp', 'seq')
- conv_grad: float32 [768, 768], P('seq')
- proj_grad: float32 [768, 256], P('seq')
All inputs are finite; a program needn't handle non-finite values.
Results may differ from a plain program's by a relative error of at most 0.015.
Values may be sent and summed in bfloat16 or wider, within the bound.
A program may use at most 64 MiB of HBM per device.

v0:
```python
import math

import jax
import jax.numpy as jnp
from jax import lax
from jax.sharding import PartitionSpec as P


def passed_along(value, axis, steps):
    count = lax.axis_size(axis)
    first, last = (max(0, -steps), min(count, count - steps))
    return lax.ppermute(value, axis, [(source, source + steps) for source in range(first, last)])


def gelu_tanh(value):
    coeff = math.sqrt(2.0 / math.pi)
    return 0.5 * value * (1.0 + jnp.tanh(coeff * (value + 0.044715 * value * value * value)))


def gelu_slope(value):
    coeff = math.sqrt(2.0 / math.pi)
    inner = jnp.tanh(coeff * (value + 0.044715 * value * value * value))
    return 0.5 * (1.0 + inner) + 0.5 * value * (1.0 - inner * inner) * coeff * (
        1.0 + 3.0 * 0.044715 * value * value
    )


def normalize(value, counted):
    totals, second = lax.psum(
        (jnp.sum(value, axis=0), jnp.sum(value * value, axis=0)), ("seq", "dp")
    )
    center = totals / counted
    squares = second / counted - center * center
    spread = jnp.sqrt(squares + 1e-05)
    return ((value - center) / spread, spread)


def back_norm(dpre, normed, gain, spread, counted):
    first, second = lax.psum((jnp.sum(dpre, axis=0), jnp.sum(dpre * normed, axis=0)), ("seq", "dp"))
    return gain * (dpre - first / counted - normed * (second / counted)) / spread


def per_device(inputs, cotangent, conv_weight, proj_weight, gain_in, bias_in, gain_mid, bias_mid):
    samples, places, width = inputs.shape
    central_window = proj_weight.shape[0]
    counted = samples * places * lax.axis_size("seq") * lax.axis_size("dp")
    stream = inputs.reshape(samples * places, width).astype(jnp.float32)
    normed_in, spread_in = normalize(stream, counted)
    pre_in = gain_in * normed_in + bias_in
    act_in = gelu_tanh(pre_in).astype(jnp.bfloat16)
    shaped = act_in.reshape(samples, places, width)
    before = passed_along(shaped, "seq", 8).reshape(samples * places, width)
    after = passed_along(shaped, "seq", -8).reshape(samples * places, width)
    dilated_filter_output = jnp.dot(
        act_in,
        conv_weight[:, central_window : 2 * central_window],
        preferred_element_type=jnp.float32,
    )
    dilated_filter_output = dilated_filter_output + jnp.dot(
        before, conv_weight[:, :central_window], preferred_element_type=jnp.float32
    )
    dilated_filter_output = dilated_filter_output + jnp.dot(
        after, conv_weight[:, 2 * central_window :], preferred_element_type=jnp.float32
    )
    normed_mid, spread_mid = normalize(dilated_filter_output, counted)
    pre_mid = gain_mid * normed_mid + bias_mid
    act_mid = gelu_tanh(pre_mid).astype(jnp.bfloat16)
    update = jnp.dot(act_mid, proj_weight, preferred_element_type=jnp.float32)
    block_out = (stream + update).astype(jnp.bfloat16).reshape(samples, places, width)
    flat_cot = cotangent.reshape(samples * places, width)
    dact_mid = lax.dot_general(
        flat_cot, proj_weight, (((1,), (1,)), ((), ())), preferred_element_type=jnp.float32
    )
    dpre_mid = dact_mid * gelu_slope(pre_mid)
    filter_output_gradient = back_norm(dpre_mid, normed_mid, gain_mid, spread_mid, counted).astype(
        jnp.bfloat16
    )
    dconv_shaped = filter_output_gradient.reshape(samples, places, central_window)
    grad_before = passed_along(dconv_shaped, "seq", 8)
    grad_after = passed_along(dconv_shaped, "seq", -8)
    stacked_windows = jnp.concatenate([grad_after, dconv_shaped, grad_before], axis=2).reshape(
        samples * places, 3 * central_window
    )
    part_conv = lax.dot_general(
        act_in, stacked_windows, (((0,), (0,)), ((), ())), preferred_element_type=jnp.float32
    )
    part_proj = lax.dot_general(
        flat_cot, act_mid, (((0,), (0,)), ((), ())), preferred_element_type=jnp.float32
    )
    shares = (
        lax.psum_scatter(part_conv, "seq", scatter_dimension=0, tiled=True),
        lax.psum_scatter(part_proj, "seq", scatter_dimension=0, tiled=True),
    )
    conv_grad, proj_grad = (
        lax.psum(shares[0].astype(jnp.bfloat16), "dp").astype(jnp.float32),
        lax.psum(shares[1].astype(jnp.bfloat16), "dp").astype(jnp.float32),
    )
    dact_in = lax.dot_general(
        stacked_windows, conv_weight, (((1,), (1,)), ((), ())), preferred_element_type=jnp.float32
    )
    dpre_in = dact_in * gelu_slope(pre_in)
    input_grad = (
        flat_cot.astype(jnp.float32) + back_norm(dpre_in, normed_in, gain_in, spread_in, counted)
    ).astype(jnp.bfloat16)
    return (block_out, input_grad.reshape(samples, places, width), conv_grad, proj_grad)


def solution(mesh):
    in_specs = (P("dp", "seq", None), P("dp", "seq", None), P(), P(), P(), P(), P(), P())
    out_specs = (P("dp", "seq", None), P("dp", "seq", None), P("seq", None), P("seq", None))
    return jax.shard_map(
        per_device, mesh=mesh, in_specs=in_specs, out_specs=out_specs, check_vma=False
    )
```

profile of v0, /device:TPU:0, one launch (start us, length us, event | category | flops | bytes accessed | tf_op | source)
XLA Modules:
  0.0 314.7 jit_solution(2179137879247069376)
XLA Ops:
  7.2 0.0 copy-start
  7.2 0.0 reduce-scatter.5.cloned.1.call-start
  7.2 1.0 convert_reduce_fusion
  8.2 1.0 fusion.5
  9.2 42.1 %all-reduce.3 = (f32[768]{0:T(1024)S(1)}, f32[768]{0:T(1024)S(1)}) all-reduce(f32[768]{0:T(1024)S(1)} %fusion.5, f32[768]{0:T(1024)S(1)} %convert_reduce_fusion), channel_id=1, replica_groups=mesh['seq'=16,'dp'=2] {'seq','dp'}, use_global_device_ids=true, to_apply=%region_3.0 | all-reduce | flops 1536 | bytes 12288 | tf_op jit(solution)/shard_map/psum | solution.py:29
  51.3 1.1 fusion.15
  52.5 0.0 copy-start.3
  52.5 4.4 %collective-permute-start = (bf16[1,128,768]{2,1,0:T(8,128)(2,1)S(1)}, bf16[1,128,768]{2,1,0:T(8,128)(2,1)S(1)}, u32[]{:S(2)}, u32[]{:S(2)}) collective-permute-start(bf16[1,128,768]{2,1,0:T(8,128)(2,1)S(1)} %fusion.15), channel_id=1, source_target_pairs={{0,16},{2,18},{4,20},{6,22},{8,24},{10,26},{12,28},{14,30},{1,17},... | collective-permute-start | bytes 589832 | tf_op jit(solution)/shard_map/ppermute | solution.py:12
  56.9 1.3 collective-permute-start.1
  58.2 1.5 fusion.21
  59.6 0.0 copy-start.2
  59.7 0.0 copy-start.6
  59.7 0.0 copy-start.7
  59.7 0.6 collective-permute-done
  60.2 0.2 convolution_add_fusion.2
  60.5 8.8 %collective-permute-done.1 = bf16[1,128,768]{2,1,0:T(8,128)(2,1)S(1)} collective-permute-done((bf16[1,128,768]{2,1,0:T(8,128)(2,1)S(1)}, bf16[1,128,768]{2,1,0:T(8,128)(2,1)S(1)}, u32[]{:S(2)}, u32[]{:S(2)}) %collective-permute-start.1) | collective-permute-done | bytes 196640 | tf_op jit(solution)/shard_map/ppermute | solution.py:12
  69.3 0.2 fusion.51
  69.5 37.7 %all-reduce.2 = (f32[256]{0:T(256)S(1)}, f32[256]{0:T(256)S(1)}) all-reduce(f32[256]{0:T(256)S(1)} %get-tuple-element.17, f32[256]{0:T(256)S(1)} %get-tuple-element.16), channel_id=1, replica_groups=mesh['seq'=16,'dp'=2] {'seq','dp'}, use_global_device_ids=true, to_apply=%region_7.0 | all-reduce | flops 512 | bytes 4096 | tf_op jit(solution)/shard_map/psum | solution.py:29
  107.3 0.0 copy-done.2
  107.3 0.0 copy-done.6
  107.3 0.0 copy-done.7
  107.3 0.3 fusion.50
  107.6 41.4 %all-reduce.1 = (f32[256]{0:T(256)S(1)}, f32[256]{0:T(256)S(1)}) all-reduce(f32[256]{0:T(256)S(1)} %get-tuple-element.15, f32[256]{0:T(256)S(1)} %get-tuple-element.14), channel_id=1, replica_groups=mesh['seq'=16,'dp'=2] {'seq','dp'}, use_global_device_ids=true, to_apply=%region_11.0 | all-reduce | flops 512 | bytes 4096 | tf_op jit(solution)/shard_map/psum | solution.py:39
  149.1 1.3 collective-permute-start.2
  150.4 5.4 %collective-permute-start.3 = (bf16[1,128,256]{2,1,0:T(8,128)(2,1)S(1)}, bf16[1,128,256]{2,1,0:T(8,128)(2,1)S(1)}, u32[]{:S(2)}, u32[]{:S(2)}) collective-permute-start(bf16[1,128,256]{2,1,0:T(8,128)(2,1)S(1)} %fusion.41), channel_id=1, source_target_pairs={{0,16},{2,18},{4,20},{6,22},{8,24},{10,26},{12,28},{14,30},{1,17},... | collective-permute-start | bytes 196616 | tf_op jit(solution)/shard_map/ppermute | solution.py:12
  155.8 0.4 collective-permute-done.2
  156.2 1.5 collective-permute-done.3
  157.7 1.9 fusion.23
  159.6 0.0 reduce-scatter.5.cloned.1.call-update
  159.7 0.0 reduce-scatter.7.cloned.1.call-start
  159.7 0.3 convolution_bitcast_fusion
  160.0 0.0 copy-start.1
  160.1 1.2 copy.14
  161.2 0.0 reduce-scatter.7.cloned.1.call-update
  161.3 0.0 all-reduce.6.cloned.1.call-start
  161.3 0.9 fusion.1
  162.2 0.6 fusion.49
  162.9 42.3 %all-reduce = (f32[768]{0:T(1024)S(1)}, f32[768]{0:T(1024)S(1)}) all-reduce(f32[768]{0:T(1024)S(1)} %get-tuple-element.13, f32[768]{0:T(1024)S(1)} %get-tuple-element.12), channel_id=1, replica_groups=mesh['seq'=16,'dp'=2] {'seq','dp'}, use_global_device_ids=true, to_apply=%region_15.0 | all-reduce | flops 1536 | bytes 12288 | tf_op jit(solution)/shard_map/psum | solution.py:39
  205.2 19.3 %reduce-scatter.5.cloned.1.call-done = f32[48,768]{1,0:T(8,128)} async-done(((f32[768,768]{1,0:T(8,128)}), f32[48,768]{1,0:T(8,128)}) %reduce-scatter.5.cloned.1.call-update) | async-done | bytes 147472 | tf_op jit(solution)/shard_map/reduce_scatter | solution.py:91
  224.5 1.6 convert_element_type.54
  226.0 0.0 all-reduce.6.cloned.1.call-update
  226.0 0.8 fusion.35
  226.9 57.2 %reduce-scatter.7.cloned.1.call-done = f32[48,256]{1,0:T(8,128)} async-done(((f32[768,256]{1,0:T(8,128)}), f32[48,256]{1,0:T(8,128)}) %reduce-scatter.7.cloned.1.call-update) | async-done | bytes 49168
  284.0 0.9 copy.15
  284.9 9.4 %psum.79 = bf16[48,256]{0,1:T(8,128)(2,1)S(1)} all-reduce(bf16[48,256]{0,1:T(8,128)(2,1)S(1)} %copy.15), channel_id=1, replica_groups=mesh['seq'=16,'dp'=2] {'dp'}, use_global_device_ids=true, to_apply=%region_19.0 | all-reduce | flops 12288 | bytes 49152 | tf_op jit(solution)/shard_map/psum | solution.py:96
  294.4 0.7 copy.13
  295.1 11.5 %all-reduce.6.cloned.1.call-done = bf16[48,768]{1,0:T(8,128)(2,1)} async-done(((bf16[48,768]{1,0:T(8,128)(2,1)}), bf16[48,768]{1,0:T(8,128)(2,1)}) %all-reduce.6.cloned.1.call-update) | async-done | bytes 73744 | tf_op jit(solution)/shard_map/psum | solution.py:95
  306.6 1.6 convert_element_type.55
  (13 shorter events, 0.1 us)
Async XLA Ops:
  7.2 100.1 %copy-start = (bf16[256,768]{1,0:T(8,128)(2,1)S(1)}, bf16[256,768]{1,0:T(8,128)(2,1)}, u32[]{:S(2)}) copy-start(bf16[256,768]{1,0:T(8,128)(2,1)} %param.11) | copy-start | bytes 1179652
  7.2 217.3 %reduce-scatter.5.cloned.1.call-start = ((), (), s32[]{:S(2)}) async-start(), calls=%async_computation.2 | async-start | bytes 2506752 | tf_op jit(solution)/shard_map/reduce_scatter | solution.py:91
  52.5 7.8 %copy-start.3 = (bf16[768,768]{1,0:T(8,128)(2,1)S(1)}, bf16[768,768]{1,0:T(8,128)(2,1)}, u32[]{:S(2)}) copy-start(bf16[768,768]{1,0:T(8,128)(2,1)} %param.10) | copy-start | bytes 3538948
  52.5 7.7 %collective-permute-start = (bf16[1,128,768]{2,1,0:T(8,128)(2,1)S(1)}, bf16[1,128,768]{2,1,0:T(8,128)(2,1)S(1)}, u32[]{:S(2)}, u32[]{:S(2)}) collective-permute-start(bf16[1,128,768]{2,1,0:T(8,128)(2,1)S(1)} %fusion.15), channel_id=1, source_target_pairs={{0,16},{2,18},{4,20},{6,22},{8,24},{10,26},{12,28},{14,30},{1,17},... | collective-permute-start | bytes 589832 | tf_op jit(solution)/shard_map/ppermute | solution.py:12
  56.9 12.4 %collective-permute-start.1 = (bf16[1,128,768]{2,1,0:T(8,128)(2,1)S(1)}, bf16[1,128,768]{2,1,0:T(8,128)(2,1)S(1)}, u32[]{:S(2)}, u32[]{:S(2)}) collective-permute-start(bf16[1,128,768]{2,1,0:T(8,128)(2,1)S(1)} %fusion.15), channel_id=1, source_target_pairs={{16,0},{18,2},{20,4},{22,6},{24,8},{26,10},{28,12},{30,14},{17,1},... | collective-permute-start | bytes 589832 | tf_op jit(solution)/shard_map/ppermute | solution.py:12
  59.6 47.6 %copy-start.2 = (bf16[1,128,768]{2,1,0:T(8,128)(2,1)S(1)}, bf16[1,128,768]{2,1,0:T(8,128)(2,1)}, u32[]{:S(2)}) copy-start(bf16[1,128,768]{2,1,0:T(8,128)(2,1)} %param.9) | copy-start | bytes 589828
  59.7 47.6 %copy-start.6 = (f32[256]{0:T(256)S(1)}, f32[256]{0:T(256)}, u32[]{:S(2)}) copy-start(f32[256]{0:T(256)} %param.14) | copy-start | bytes 3076
  59.7 47.6 %copy-start.7 = (f32[256]{0:T(256)S(1)}, f32[256]{0:T(256)}, u32[]{:S(2)}) copy-start(f32[256]{0:T(256)} %param.15) | copy-start | bytes 3076
  149.1 7.1 %collective-permute-start.2 = (bf16[1,128,256]{2,1,0:T(8,128)(2,1)S(1)}, bf16[1,128,256]{2,1,0:T(8,128)(2,1)S(1)}, u32[]{:S(2)}, u32[]{:S(2)}) collective-permute-start(bf16[1,128,256]{2,1,0:T(8,128)(2,1)S(1)} %fusion.41), channel_id=1, source_target_pairs={{16,0},{18,2},{20,4},{22,6},{24,8},{26,10},{28,12},{30,14},{17,1},... | collective-permute-start | bytes 196616 | tf_op jit(solution)/shard_map/ppermute | solution.py:12
  150.4 7.3 %collective-permute-start.3 = (bf16[1,128,256]{2,1,0:T(8,128)(2,1)S(1)}, bf16[1,128,256]{2,1,0:T(8,128)(2,1)S(1)}, u32[]{:S(2)}, u32[]{:S(2)}) collective-permute-start(bf16[1,128,256]{2,1,0:T(8,128)(2,1)S(1)} %fusion.41), channel_id=1, source_target_pairs={{0,16},{2,18},{4,20},{6,22},{8,24},{10,26},{12,28},{14,30},{1,17},... | collective-permute-start | bytes 196616 | tf_op jit(solution)/shard_map/ppermute | solution.py:12
  159.7 124.4 %reduce-scatter.7.cloned.1.call-start = ((), (), s32[]{:S(2)}) async-start(), calls=%async_computation.4 | async-start | bytes 835584
  160.0 1.3 copy-start.1
  161.2 1.0 copy-start.4
  161.2 1.0 copy-start.5
  161.3 145.4 %all-reduce.6.cloned.1.call-start = ((), (), s32[]{:S(2)}) async-start(), calls=%async_computation.3 | async-start | bytes 147456 | tf_op jit(solution)/shard_map/psum | solution.py:95
Sparse Core Ops, SparseCore 0:
  159.8 64.6 reduce-scatter.4
  228.4 55.5 reduce-scatter.6
  286.9 19.7 all-reduce.5
where the time goes:
time: 316 us; the launch traced here: 315 us
  blocking collectives  173 us (55%)
  waiting for transfers between devices  99.3 us (31%)
  between operations  13.9 us (4%)
  starting transfers between devices  12.5 us (4%)
  other arithmetic  7.14 us (2%)
  matrix products  6.06 us (2%)
    psum x2, blocking collectives, back_norm(): lax.psum((jnp.sum(dpre, axis=0), jnp.sum(dpre * normed, axis=0)), ('seq',...  83.7 us
    psum x2, blocking collectives, normalize(): lax.psum((jnp.sum(value, axis=0), jnp.sum(value * value, axis=0)), ('seq'...  79.8 us
    unnamed x4, waiting for transfers between devices  57.2 us
    reduce_scatter x1, waiting for transfers between devices, per_device(): lax.psum_scatter(part_conv, 'seq', scatter_dimension=0, tiled=True)  19.3 us
    ppermute x4, starting transfers between devices, passed_along(): lax.ppermute(value, axis, [(source, source + steps) for source in range(f...  12.4 us
    psum x1, waiting for transfers between devices, per_device(): lax.psum(shares[0].astype(jnp.bfloat16), 'dp').astype(jnp.float32)  11.5 us
    ppermute x4, waiting for transfers between devices, passed_along(): lax.ppermute(value, axis, [(source, source + steps) for source in range(f...  11.3 us
    psum x1, blocking collectives, per_device(): lax.psum(shares[1].astype(jnp.bfloat16), 'dp').astype(jnp.float32)  9.4 us
  transfers between devices with their start and end apart: 7, of which 7 were waited for; matrix products, arithmetic and copies ran while one was open for 3% of the time, Pallas kernels for 0%

commit v1 on v0

v1 whole, which is shorter than its diff:
```python
import functools
import math

import jax
import jax.numpy as jnp
from jax import lax
from jax.experimental import pallas as pl
from jax.experimental.pallas import tpu as pltpu
from jax.sharding import PartitionSpec as P

DILATION = 1024
EPS = 1e-05
COEFF = math.sqrt(2.0 / math.pi)
MESH = pl.DeviceIdType.MESH
F32, BF16 = jnp.float32, jnp.bfloat16


def gelu_inner(v):
    return jnp.tanh(COEFF * (v + 0.044715 * v * v * v))


def gelu_slope(v, inner):
    return 0.5 * (1.0 + inner) + 0.5 * v * (1.0 - inner * inner) * COEFF * (
        1.0 + 3.0 * 0.044715 * v * v
    )


def dot(a, b):
    return jnp.dot(a, b, preferred_element_type=F32)


def dot_t(a, b):
    return lax.dot_general(a, b, (((1,), (1,)), ((), ())), preferred_element_type=F32)


def column_sums(a, b):
    return jnp.concatenate(
        [jnp.sum(a, axis=0, keepdims=True), jnp.sum(b, axis=0, keepdims=True)], axis=0
    )


class Plan:
    def __init__(self, n, m, samples, places, width, mid):
        self.n, self.m = n, m
        self.rows, self.width, self.mid = samples * places, width, mid
        self.counted = float(samples * places * n * m)
        steps = DILATION // places
        inner = 2
        while inner * inner < n:
            inner *= 2
        self.inner, self.nz, self.nx = inner, n // inner, inner // 2
        assert steps % inner == 0 and n % inner == 0
        self.hz = steps // inner
        assert 0 < self.hz < self.nz
        self.block = width // n
        self.padded = -(-self.block // 16) * 16
        if inner * m <= 8:
            self.phases = ("plane", "z")
        else:
            self.phases = ("lo", "dp", "z")
        size = {"plane": inner * m, "lo": inner, "dp": m, "z": self.nz}
        self.sizes = [size[p] for p in self.phases]
        self.slots = sum(s - 1 for s in self.sizes)
        q = self.nz * 2 - 1
        self.sems = 4 * self.slots + 4 * q + self.nx * m - 1 + 2


def kernel(
    plan,
    x_ref, cot_ref, cw_ref, pw_ref, gi_ref, bi_ref, gm_ref, bm_ref,
    out_ref, grad_ref, convg_ref, projg_ref,
    src_w, src_m, got_w, got_m,
    act, h1, pre1, inner1, dact2, before, after, ysend, dact1,
    cot_t, act_t, cot_all, act_all, act2_all, dconv_all, part, parts,
    send_sem, recv_sem, local_sem,
):
    n, m, nz, nx, inner = plan.n, plan.m, plan.nz, plan.nx, plan.inner
    rows, mid, width, block, padded = plan.rows, plan.mid, plan.width, plan.block, plan.padded
    me, dp = lax.axis_index("seq"), lax.axis_index("dp")
    z, lo = lax.div(me, inner), lax.rem(me, inner)
    xi, core = lax.div(lo, 2), lax.rem(lo, 2)
    counter = [0]
    pending = []

    def copy_to(src, dst, target):
        k = counter[0]
        counter[0] += 1
        return pltpu.make_async_remote_copy(
            src_ref=src, dst_ref=dst, send_sem=send_sem.at[k], recv_sem=recv_sem.at[k],
            device_id=target, device_id_type=MESH,
        )

    def push(src, dst, target):
        c = copy_to(src, dst, target)
        c.start()
        pending.append(c)
        return c

    def plane_peer(o):
        j = lax.rem(lo * m + dp + o, inner * m)
        return (z * inner + lax.div(j, m), lax.rem(j, m))

    def z_peer(o, c=None):
        c = core if c is None else c
        return (lax.rem(z + o, nz) * inner + xi * 2 + c, dp)

    peers = {
        "plane": plane_peer,
        "lo": lambda o: (z * inner + lax.rem(lo + o, inner), dp),
        "dp": lambda o: (me, lax.rem(dp + o, m)),
        "z": z_peer,
    }
    core_peer = (z * inner + xi * 2 + (1 - core), dp)

    def reduce_start(src, got, which):
        state = dict(src=src, got=got, which=which, phase=0, base=0)
        launch(state)
        return state

    def launch(st):
        ph = st["phase"]
        st["copies"] = [
            push(st["src"].at[st["which"], ph], st["got"].at[st["which"], st["base"] + o - 1],
                 peers[plan.phases[ph]](o))
            for o in range(1, plan.sizes[ph])
        ]

    def collect(st):
        ph = st["phase"]
        total = st["src"][st["which"], ph]
        for i, c in enumerate(st["copies"]):
            c.wait_recv()
            total = total + st["got"][st["which"], st["base"] + i]
        st["base"] += plan.sizes[ph] - 1
        st["phase"] += 1
        return total

    def reduce_step(st):
        total = collect(st)
        st["src"][st["which"], st["phase"]] = total
        launch(st)

    def reduce_mid(st):
        while st["phase"] < len(plan.phases) - 1:
            reduce_step(st)

    def reduce_end(st):
        reduce_mid(st)
        return collect(st) / plan.counted

    barrier = pltpu.get_barrier_semaphore()
    friends = [plane_peer(o) for o in range(1, inner * m)]
    friends += [z_peer(o, c) for o in range(1, nz) for c in (core, 1 - core)]
    for f in friends:
        pl.semaphore_signal(barrier, inc=1, device_id=f, device_id_type=MESH)

    x = x_ref[...].astype(F32)
    src_w[0, 0] = column_sums(x, x * x)
    pl.semaphore_wait(barrier, len(friends))
    red = reduce_start(src_w, got_w, 0)

    def spread_columns(value, staged, gathered):
        turned = value.T
        if padded != block:
            staged[...] = jnp.zeros_like(staged)
        for i in range(n):
            staged[i // inner, (i % inner) // 2, i % 2, :block, :] = turned[
                i * block : (i + 1) * block, :
            ].astype(BF16)
        q = z * 2 + core
        lanes = pl.ds(pl.multiple_of(q * rows, rows), rows)
        copies = []
        for o in range(nz):
            for c in (core, 1 - core):
                if o == 0 and c is core:
                    continue
                copies.append(
                    push(staged.at[lax.rem(z + o, nz), :, c], gathered.at[:, :, lanes], z_peer(o, c))
                )
        return copies, (staged.at[z, :, core], gathered.at[:, :, lanes])

    cot = cot_ref[...]
    dact2[...] = dot_t(cot, pw_ref[...])
    cot_copies, cot_own = spread_columns(cot.astype(F32), cot_t, cot_all)
    own_cot = pltpu.make_async_copy(*cot_own, local_sem.at[0])
    own_cot.start()

    mean = reduce_end(red)
    center = mean[0:1]
    rs1 = 1.0 / jnp.sqrt(mean[1:2] - center * center + EPS)
    h = (x_ref[...].astype(F32) - center) * rs1
    h1[...] = h
    pre = gi_ref[...] * h + bi_ref[...]
    t = gelu_inner(pre)
    pre1[...] = pre
    inner1[...] = t
    act[...] = (0.5 * pre * (1.0 + t)).astype(BF16)

    steps = plan.hz * inner
    up = copy_to(ysend.at[0], before, (lax.rem(me + steps, n), dp))
    down = copy_to(ysend.at[1], after, (lax.rem(me + n - steps, n), dp))
    has_next, has_prev = me < n - steps, me >= steps

    @pl.when(has_next)
    def _():
        ysend[0] = dot(act[...], cw_ref[:, :mid]).astype(BF16)
        up.start()

    @pl.when(has_prev)
    def _():
        ysend[1] = dot(act[...], cw_ref[:, 2 * mid :]).astype(BF16)
        down.start()

    conv = dot(act[...], cw_ref[:, mid : 2 * mid])
    act_copies, act_own = spread_columns(act[...].astype(F32), act_t, act_all)
    own_act = pltpu.make_async_copy(*act_own, local_sem.at[1])
    own_act.start()

    @pl.when(has_prev)
    def _():
        up.wait_recv()

    @pl.when(jnp.logical_not(has_prev))
    def _():
        before[...] = jnp.zeros_like(before)

    @pl.when(has_next)
    def _():
        down.wait_recv()

    @pl.when(jnp.logical_not(has_next))
    def _():
        after[...] = jnp.zeros_like(after)

    conv = conv + before[...].astype(F32) + after[...].astype(F32)
    src_m[0, 0] = column_sums(conv, conv * conv)
    mean = reduce_end(reduce_start(src_m, got_m, 0))
    center = mean[0:1]
    rs2 = 1.0 / jnp.sqrt(mean[1:2] - center * center + EPS)
    h2 = (conv - center) * rs2
    pre2 = gm_ref[...] * h2 + bm_ref[...]
    t2 = gelu_inner(pre2)
    act2 = (0.5 * pre2 * (1.0 + t2)).astype(BF16)
    dpre2 = dact2[...] * gelu_slope(pre2, t2)
    src_m[1, 0] = column_sums(dpre2, dpre2 * h2)
    red = reduce_start(src_m, got_m, 1)

    def place(zz, c):
        return pl.ds(pl.multiple_of((zz * 2 + c) * rows, rows), rows)

    own = place(z, core)

    def gather_start(full):
        order = sorted(range(1, nz), key=lambda o: o not in (plan.hz, nz - plan.hz))
        over_z = {o: push(full.at[own], full.at[own], z_peer(o)) for o in order}
        return over_z, [push(full.at[own], full.at[own], core_peer)]

    def pass_on(full, over_z, across, o):
        over_z[o].wait_recv()
        piece = full.at[place(lax.rem(z + nz - o, nz), core)]
        across.append(push(piece, piece, core_peer))

    act2_all[own, :] = act2
    act2_z, act2_c = gather_start(act2_all)
    out_ref[...] = (x_ref[...].astype(F32) + dot(act2, pw_ref[...])).astype(BF16)
    mean = reduce_end(red)
    dconv = (gm_ref[...] * (dpre2 - mean[0:1] - h2 * mean[1:2]) * rs2).astype(BF16)
    dconv_all[own, :] = dconv
    dconv_z, dconv_c = gather_start(dconv_all)
    dact1[...] = dot_t(dconv, cw_ref[:, mid : 2 * mid])
    slope1 = gelu_slope(pre1[...], inner1[...])
    pre1[...] = slope1
    halo = sorted({plan.hz, nz - plan.hz})
    for o in halo:
        pass_on(dconv_all, dconv_z, dconv_c, o)

    @pl.when(z + plan.hz < nz)
    def _():
        dact1[...] += dot_t(
            dconv_all[place(lax.rem(z + plan.hz, nz), core), :], cw_ref[:, :mid]
        )

    @pl.when(z >= plan.hz)
    def _():
        dact1[...] += dot_t(
            dconv_all[place(lax.rem(z + nz - plan.hz, nz), core), :], cw_ref[:, 2 * mid :]
        )

    dpre1 = dact1[...] * pre1[...]
    dact1[...] = dpre1
    src_w[1, 0] = column_sums(dpre1, dpre1 * h1[...])
    red = reduce_start(src_w, got_w, 1)

    for o in range(1, nz):
        pass_on(act2_all, act2_z, act2_c, o)
    reduce_mid(red)
    for o in range(1, nz):
        if o not in halo:
            pass_on(dconv_all, dconv_z, dconv_c, o)
    own_cot.wait()
    own_act.wait()
    for c in cot_copies + act_copies + act2_c + dconv_c:
        c.wait_recv()

    depth = nz * 2 * rows
    shift = plan.hz * 2 * rows
    for k in range(nx):
        part[k, :, :mid] = dot(
            act_all[k, :, : depth - shift], dconv_all[shift:, :]
        ).astype(BF16)
        part[k, :, mid : 2 * mid] = dot(act_all[k], dconv_all[...]).astype(BF16)
        part[k, :, 2 * mid : 3 * mid] = dot(
            act_all[k, :, shift:], dconv_all[: depth - shift, :]
        ).astype(BF16)
        part[k, :, 3 * mid :] = dot(cot_all[k], act2_all[...]).astype(BF16)
    group = nx * m
    mine = xi * m + dp
    part_copies = []
    for o in range(1, group):
        to = lax.rem(mine + o, group)
        tx, ty = lax.div(to, m), lax.rem(to, m)
        part_copies.append(
            push(part.at[tx], parts.at[mine], (z * inner + tx * 2 + core, ty))
        )
    parts[pl.ds(mine, 1)] = part[pl.ds(xi, 1)]

    mean = reduce_end(red)
    grad_ref[...] = (
        cot_ref[...].astype(F32)
        + gi_ref[...] * (dact1[...] - mean[0:1] - h1[...] * mean[1:2]) * rs1
    ).astype(BF16)

    for c in part_copies:
        c.wait_recv()
    total = parts[0].astype(F32)
    for k in range(1, group):
        total = total + parts[k].astype(F32)
    convg_ref[...] = total[:block, : 3 * mid]
    projg_ref[...] = total[:block, 3 * mid :]

    for c in pending:
        c.wait_send()

    @pl.when(has_next)
    def _():
        up.wait_send()

    @pl.when(has_prev)
    def _():
        down.wait_send()


def per_device(inputs, cotangent, conv_weight, proj_weight, gain_in, bias_in, gain_mid, bias_mid):
    samples, places, width = inputs.shape
    mid = proj_weight.shape[0]
    plan = Plan(
        lax.axis_size("seq"), lax.axis_size("dp"), samples, places, width, mid
    )
    rows, nz, nx, padded = plan.rows, plan.nz, plan.nx, plan.padded
    depth = nz * 2 * rows
    vmem = pl.BlockSpec(memory_space=pltpu.VMEM)
    phases = len(plan.phases)
    block_out, input_grad, conv_grad, proj_grad = pl.pallas_call(
        functools.partial(kernel, plan),
        out_shape=(
            jax.ShapeDtypeStruct((rows, width), BF16),
            jax.ShapeDtypeStruct((rows, width), BF16),
            jax.ShapeDtypeStruct((plan.block, 3 * mid), F32),
            jax.ShapeDtypeStruct((plan.block, mid), F32),
        ),
        in_specs=[vmem] * 8,
        out_specs=(vmem,) * 4,
        scratch_shapes=[
            pltpu.VMEM((2, phases, 2, width), F32),
            pltpu.VMEM((2, phases, 2, mid), F32),
            pltpu.VMEM((2, plan.slots, 2, width), F32),
            pltpu.VMEM((2, plan.slots, 2, mid), F32),
            pltpu.VMEM((rows, width), BF16),
            pltpu.VMEM((rows, width), F32),
            pltpu.VMEM((rows, width), F32),
            pltpu.VMEM((rows, width), F32),
            pltpu.VMEM((rows, mid), F32),
            pltpu.VMEM((rows, mid), BF16),
            pltpu.VMEM((rows, mid), BF16),
            pltpu.VMEM((2, rows, mid), BF16),
            pltpu.VMEM((rows, width), F32),
            pltpu.VMEM((nz, nx, 2, padded, rows), BF16),
            pltpu.VMEM((nz, nx, 2, padded, rows), BF16),
            pltpu.VMEM((nx, padded, depth), BF16),
            pltpu.VMEM((nx, padded, depth), BF16),
            pltpu.VMEM((depth, mid), BF16),
            pltpu.VMEM((depth, mid), BF16),
            pltpu.VMEM((nx, padded, 4 * mid), BF16),
            pltpu.VMEM((nx * plan.m, padded, 4 * mid), BF16),
            pltpu.SemaphoreType.DMA((plan.sems,)),
            pltpu.SemaphoreType.DMA((plan.sems,)),
            pltpu.SemaphoreType.DMA((2,)),
        ],
        compiler_params=pltpu.CompilerParams(
            collective_id=0, has_side_effects=True, vmem_limit_bytes=32 * 1024 * 1024
        ),
    )(
        inputs.reshape(rows, width),
        cotangent.reshape(rows, width),
        conv_weight,
        proj_weight,
        gain_in.reshape(1, width),
        bias_in.reshape(1, width),
        gain_mid.reshape(1, mid),
        bias_mid.reshape(1, mid),
    )
    shape = (samples, places, width)
    return (block_out.reshape(shape), input_grad.reshape(shape), conv_grad, proj_grad)


def solution(mesh):
    in_specs = (P("dp", "seq", None), P("dp", "seq", None), P(), P(), P(), P(), P(), P())
    out_specs = (P("dp", "seq", None), P("dp", "seq", None), P("seq", None), P("seq", None))
    return jax.shard_map(
        per_device, mesh=mesh, in_specs=in_specs, out_specs=out_specs, check_vma=False
    )
```

time: 316 us -> 63.5 us (0.20)
  blocking collectives: 173 us -> 0 us
  waiting for transfers between devices: 99.3 us -> 0 us
  Pallas kernels: 0 us -> 53.1 us
  between operations: 13.9 us -> 0.65 us
  starting transfers between devices: 12.5 us -> 0 us
  other arithmetic: 7.14 us -> 0 us
  local copies, waits for them, and re-layouts: 2.84 us -> 9.49 us
  matrix products: 6.06 us -> 0 us
    psum x5 -> x0, blocking collectives: 173 us -> none  [the longest x2 83.7 us: back_norm(): lax.psum((jnp.sum(dpre, axis=0), jnp.sum(dpre * normed, axis=0)), ('seq',...]
    unnamed x4 -> x0, waiting for transfers between devices: 57.2 us -> none
    pallas_call x0 -> x1, Pallas kernels: none -> 53.1 us  [per_device(): pl.pallas_call(functools.partial(kernel, plan), out_shape=(jax.ShapeDtype...]
    reduce_scatter x1 -> x0, waiting for transfers between devices: 19.3 us -> none  [per_device(): lax.psum_scatter(part_conv, 'seq', scatter_dimension=0, tiled=True)]
    ppermute x4 -> x0, starting transfers between devices: 12.4 us -> none  [passed_along(): lax.ppermute(value, axis, [(source, source + steps) for source in range(f...]
    psum x1 -> x0, waiting for transfers between devices: 11.5 us -> none  [per_device(): lax.psum(shares[0].astype(jnp.bfloat16), 'dp').astype(jnp.float32)]
    ppermute x4 -> x0, waiting for transfers between devices: 11.3 us -> none  [passed_along(): lax.ppermute(value, axis, [(source, source + steps) for source in range(f...]
    dot_general x8 -> x0, matrix products: 6.06 us -> none  [the longest x1 1.91 us: per_device(): lax.dot_general(act_in, stacked_windows, (((0,), (0,)), ((), ())), prefer...]
  transfers between devices with their start and end apart: 7 -> 0, of which waited for: 7 -> 0; matrix products, arithmetic and copies ran while one was open for 3% -> 0% of each run, Pallas kernels for 0% -> 0%
where the time goes in v1:
time: 63.5 us; the launch traced here: 63.2 us
  Pallas kernels  53.1 us (84%)
  local copies, waits for them, and re-layouts  9.49 us (15%)
  between operations  0.65 us (1%)
    pallas_call x1, Pallas kernels, per_device(): pl.pallas_call(functools.partial(kernel, plan), out_shape=(jax.ShapeDtype...  53.1 us
    unnamed x16, local copies, waits for them, and re-layouts  8.11 us

profile of v1, /device:TPU:0, one launch (start us, length us, event | category | flops | bytes accessed | tf_op | source)
XLA Modules:
  0.0 63.2 jit_solution(9448206147211674646)
XLA Ops:
  0.6 0.7 %reshape.34.gi_ref = f32[1,768]{1,0:T(1,128)S(1)} reshape(f32[768]{0:T(1024)} %param.12) | data formatting | bytes 6144 | tf_op jit(solution)/shard_map/reshape | solution.py:407
  1.3 0.7 %reshape.35.bi_ref = f32[1,768]{1,0:T(1,128)S(1)} reshape(f32[768]{0:T(1024)} %param.13) | data formatting | bytes 6144 | tf_op jit(solution)/shard_map/reshape | solution.py:408
  2.0 0.0 copy-start
  2.0 1.3 %copy-done = bf16[768,768]{1,0:T(8,128)(2,1)S(1)} copy-done((bf16[768,768]{1,0:T(8,128)(2,1)S(1)}, bf16[768,768]{1,0:T(8,128)(2,1)}, u32[]{:S(2)}) %copy-start) | copy-done | bytes 1179672
  3.3 0.0 copy-start.1
  3.3 1.0 %copy-done.1 = bf16[256,768]{1,0:T(8,128)(2,1)S(1)} copy-done((bf16[256,768]{1,0:T(8,128)(2,1)S(1)}, bf16[256,768]{1,0:T(8,128)(2,1)}, u32[]{:S(2)}) %copy-start.1) | copy-done | bytes 393240
  4.3 0.0 copy-start.2
  4.3 0.9 %copy-done.2 = bf16[1,128,768]{2,1,0:T(8,128)(2,1)S(1)} copy-done((bf16[1,128,768]{2,1,0:T(8,128)(2,1)S(1)}, bf16[1,128,768]{2,1,0:T(8,128)(2,1)}, u32[]{:S(2)}) %copy-start.2) | copy-done | bytes 196632
  5.2 0.0 copy-start.3
  5.2 0.9 %copy-done.3 = bf16[1,128,768]{2,1,0:T(8,128)(2,1)S(1)} copy-done((bf16[1,128,768]{2,1,0:T(8,128)(2,1)S(1)}, bf16[1,128,768]{2,1,0:T(8,128)(2,1)}, u32[]{:S(2)}) %copy-start.3) | copy-done | bytes 196632
  6.1 0.0 copy-start.4
  6.1 0.7 %copy-done.4 = f32[256]{0:T(256)S(1)} copy-done((f32[256]{0:T(256)S(1)}, f32[256]{0:T(256)}, u32[]{:S(2)}) %copy-start.4) | copy-done | bytes 1048
  6.8 0.0 copy-start.5
  6.8 0.7 %copy-done.5 = f32[256]{0:T(256)S(1)} copy-done((f32[256]{0:T(256)S(1)}, f32[256]{0:T(256)}, u32[]{:S(2)}) %copy-start.5) | copy-done | bytes 1048
  7.5 53.1 %shard_map.111 = (bf16[128,768]{1,0:T(8,128)(2,1)S(1)}, bf16[128,768]{1,0:T(8,128)(2,1)S(1)}, f32[48,768]{1,0:T(8,128)S(1)}, f32[48,256]{1,0:T(8,128)S(1)}) custom-call(bf16[128,768]{1,0:T(8,128)(2,1)S(1)} %bitcast.8, bf16[128,768]{1,0:T(8,128)(2,1)S(1)} %bitcast.9, bf16[768,768]{1,0:T(8,128)(2,1)S(1)} %copy-done, bf16[256,768]{1,0:T(8,128)(2,1)S(1)} %copy-done.1, ...), custom_call_target="tpu_custom_call" | custom-call | tf_op jit(solution)/shard_map/pallas_call | solution.py:363
  60.6 0.7 %copy.16 = bf16[1,128,768]{2,1,0:T(8,128)(2,1)} copy(bf16[1,128,768]{2,1,0:T(8,128)(2,1)S(1)} %bitcast.7) | data formatting | bytes 393216
  61.2 0.7 %copy.17 = bf16[1,128,768]{2,1,0:T(8,128)(2,1)} copy(bf16[1,128,768]{2,1,0:T(8,128)(2,1)S(1)} %bitcast.6) | data formatting | bytes 393216
  61.9 0.7 %copy.18 = f32[48,768]{1,0:T(8,128)} copy(f32[48,768]{1,0:T(8,128)S(1)} %get-tuple-element.18) | data formatting | bytes 294912
  62.6 0.6 copy.19
Async XLA Ops:
  2.0 1.3 %copy-start = (bf16[768,768]{1,0:T(8,128)(2,1)S(1)}, bf16[768,768]{1,0:T(8,128)(2,1)}, u32[]{:S(2)}) copy-start(bf16[768,768]{1,0:T(8,128)(2,1)} %cw_ref.1) | copy-start | bytes 3538948
  3.3 1.0 %copy-start.1 = (bf16[256,768]{1,0:T(8,128)(2,1)S(1)}, bf16[256,768]{1,0:T(8,128)(2,1)}, u32[]{:S(2)}) copy-start(bf16[256,768]{1,0:T(8,128)(2,1)} %pw_ref.1) | copy-start | bytes 1179652
  4.3 0.9 %copy-start.2 = (bf16[1,128,768]{2,1,0:T(8,128)(2,1)S(1)}, bf16[1,128,768]{2,1,0:T(8,128)(2,1)}, u32[]{:S(2)}) copy-start(bf16[1,128,768]{2,1,0:T(8,128)(2,1)} %param.8) | copy-start | bytes 589828
  5.2 0.9 %copy-start.3 = (bf16[1,128,768]{2,1,0:T(8,128)(2,1)S(1)}, bf16[1,128,768]{2,1,0:T(8,128)(2,1)}, u32[]{:S(2)}) copy-start(bf16[1,128,768]{2,1,0:T(8,128)(2,1)} %param.9) | copy-start | bytes 589828
  6.1 0.7 %copy-start.4 = (f32[256]{0:T(256)S(1)}, f32[256]{0:T(256)}, u32[]{:S(2)}) copy-start(f32[256]{0:T(256)} %param.14) | copy-start | bytes 3076
  6.8 0.7 %copy-start.5 = (f32[256]{0:T(256)S(1)}, f32[256]{0:T(256)}, u32[]{:S(2)}) copy-start(f32[256]{0:T(256)} %param.15) | copy-start | bytes 3076

commit v2 on v1

--- a/solution.py
+++ b/solution.py
@@ -55,18 +55,20 @@
         self.block = width // n
         self.padded = -(-self.block // 16) * 16
         if inner * m <= 8:
-            self.phases = ("plane", "z")
+            self.phases = ("z", "plane")
         else:
-            self.phases = ("lo", "dp", "z")
+            self.phases = ("z", "lo", "dp")
         size = {"plane": inner * m, "lo": inner, "dp": m, "z": self.nz}
         self.sizes = [size[p] for p in self.phases]
         self.slots = sum(s - 1 for s in self.sizes)
         q = self.nz * 2 - 1
-        self.sems = 4 * self.slots + 4 * q + self.nx * m - 1 + 2
+        self.sems = 4 * self.slots + 4 * q + 2 * (self.nx * m - 1) + 2
 
 
 def kernel(
     plan,
+    x_hbm, cot_hbm, cw_hbm, pw_hbm, gi_hbm, bi_hbm, gm_hbm, bm_hbm,
+    out_hbm, grad_hbm, convg_hbm, projg_hbm,
     x_ref, cot_ref, cw_ref, pw_ref, gi_ref, bi_ref, gm_ref, bm_ref,
     out_ref, grad_ref, convg_ref, projg_ref,
     src_w, src_m, got_w, got_m,
@@ -79,6 +81,26 @@
     me, dp = lax.axis_index("seq"), lax.axis_index("dp")
     z, lo = lax.div(me, inner), lax.rem(me, inner)
     xi, core = lax.div(lo, 2), lax.rem(lo, 2)
+    loads = [
+        pltpu.make_async_copy(a, b, local_sem.at[2 + i])
+        for i, (a, b) in enumerate(
+            (
+                (x_hbm, x_ref), (cot_hbm, cot_ref), (pw_hbm, pw_ref), (gi_hbm, gi_ref),
+                (bi_hbm, bi_ref), (cw_hbm, cw_ref), (gm_hbm, gm_ref), (bm_hbm, bm_ref),
+            )
+        )
+    ]
+    stores = [
+        pltpu.make_async_copy(a, b, local_sem.at[10 + i])
+        for i, (a, b) in enumerate(
+            (
+                (out_ref, out_hbm), (grad_ref, grad_hbm),
+                (convg_ref, convg_hbm), (projg_ref, projg_hbm),
+            )
+        )
+    ]
+    for c in loads:
+        c.start()
     counter = [0]
     pending = []
 
@@ -154,12 +176,13 @@
     for f in friends:
         pl.semaphore_signal(barrier, inc=1, device_id=f, device_id_type=MESH)
 
+    loads[0].wait()
     x = x_ref[...].astype(F32)
     src_w[0, 0] = column_sums(x, x * x)
     pl.semaphore_wait(barrier, len(friends))
     red = reduce_start(src_w, got_w, 0)
 
-    def spread_columns(value, staged, gathered):
+    def stage_columns(value, staged):
         turned = value.T
         if padded != block:
             staged[...] = jnp.zeros_like(staged)
@@ -167,8 +190,12 @@
             staged[i // inner, (i % inner) // 2, i % 2, :block, :] = turned[
                 i * block : (i + 1) * block, :
             ].astype(BF16)
+
+    def spread_columns(staged, gathered, sem):
         q = z * 2 + core
         lanes = pl.ds(pl.multiple_of(q * rows, rows), rows)
+        own = pltpu.make_async_copy(staged.at[z, :, core], gathered.at[:, :, lanes], sem)
+        own.start()
         copies = []
         for o in range(nz):
             for c in (core, 1 - core):
@@ -177,20 +204,24 @@
                 copies.append(
                     push(staged.at[lax.rem(z + o, nz), :, c], gathered.at[:, :, lanes], z_peer(o, c))
                 )
-        return copies, (staged.at[z, :, core], gathered.at[:, :, lanes])
-
+        return copies, own
+
+    loads[1].wait()
+    loads[2].wait()
     cot = cot_ref[...]
-    dact2[...] = dot_t(cot, pw_ref[...])
-    cot_copies, cot_own = spread_columns(cot.astype(F32), cot_t, cot_all)
-    own_cot = pltpu.make_async_copy(*cot_own, local_sem.at[0])
-    own_cot.start()
+    stage_columns(cot.astype(F32), cot_t)
+    reduce_step(red)
+    cot_copies, own_cot = spread_columns(cot_t, cot_all, local_sem.at[0])
+    dact2[...] = dot_t(cot_ref[...], pw_ref[...])
+    for c in loads[3:]:
+        c.wait()
 
     mean = reduce_end(red)
     center = mean[0:1]
     rs1 = 1.0 / jnp.sqrt(mean[1:2] - center * center + EPS)
     h = (x_ref[...].astype(F32) - center) * rs1
     h1[...] = h
-    pre = gi_ref[...] * h + bi_ref[...]
+    pre = gi_ref[...].reshape(1, -1) * h + bi_ref[...].reshape(1, -1)
     t = gelu_inner(pre)
     pre1[...] = pre
     inner1[...] = t
@@ -212,9 +243,7 @@
         down.start()
 
     conv = dot(act[...], cw_ref[:, mid : 2 * mid])
-    act_copies, act_own = spread_columns(act[...].astype(F32), act_t, act_all)
-    own_act = pltpu.make_async_copy(*act_own, local_sem.at[1])
-    own_act.start()
+    stage_columns(act[...].astype(F32), act_t)
 
     @pl.when(has_prev)
     def _():
@@ -234,11 +263,15 @@
 
     conv = conv + before[...].astype(F32) + after[...].astype(F32)
     src_m[0, 0] = column_sums(conv, conv * conv)
-    mean = reduce_end(reduce_start(src_m, got_m, 0))
+    red = reduce_start(src_m, got_m, 0)
+    pre1[...] = gelu_slope(pre1[...], inner1[...])
+    reduce_step(red)
+    act_copies, own_act = spread_columns(act_t, act_all, local_sem.at[1])
+    mean = reduce_end(red)
     center = mean[0:1]
     rs2 = 1.0 / jnp.sqrt(mean[1:2] - center * center + EPS)
     h2 = (conv - center) * rs2
-    pre2 = gm_ref[...] * h2 + bm_ref[...]
+    pre2 = gm_ref[...].reshape(1, -1) * h2 + bm_ref[...].reshape(1, -1)
     t2 = gelu_inner(pre2)
     act2 = (0.5 * pre2 * (1.0 + t2)).astype(BF16)
     dpre2 = dact2[...] * gelu_slope(pre2, t2)
@@ -261,15 +294,17 @@
         across.append(push(piece, piece, core_peer))
 
     act2_all[own, :] = act2
+    reduce_step(red)
     act2_z, act2_c = gather_start(act2_all)
     out_ref[...] = (x_ref[...].astype(F32) + dot(act2, pw_ref[...])).astype(BF16)
+    stores[0].start()
     mean = reduce_end(red)
-    dconv = (gm_ref[...] * (dpre2 - mean[0:1] - h2 * mean[1:2]) * rs2).astype(BF16)
+    dconv = (gm_ref[...].reshape(1, -1) * (dpre2 - mean[0:1] - h2 * mean[1:2]) * rs2).astype(BF16)
     dconv_all[own, :] = dconv
     dconv_z, dconv_c = gather_start(dconv_all)
     dact1[...] = dot_t(dconv, cw_ref[:, mid : 2 * mid])
-    slope1 = gelu_slope(pre1[...], inner1[...])
-    pre1[...] = slope1
+    for o in range(1, nz):
+        pass_on(act2_all, act2_z, act2_c, o)
     halo = sorted({plan.hz, nz - plan.hz})
     for o in halo:
         pass_on(dconv_all, dconv_z, dconv_c, o)
@@ -291,15 +326,36 @@
     src_w[1, 0] = column_sums(dpre1, dpre1 * h1[...])
     red = reduce_start(src_w, got_w, 1)
 
-    for o in range(1, nz):
-        pass_on(act2_all, act2_z, act2_c, o)
+    group = nx * m
+    mine = xi * m + dp
+
+    def send_parts(columns):
+        copies = []
+        for o in range(1, group):
+            to = lax.rem(mine + o, group)
+            tx, ty = lax.div(to, m), lax.rem(to, m)
+            copies.append(
+                push(
+                    part.at[tx, :, columns],
+                    parts.at[mine, :, columns],
+                    (z * inner + tx * 2 + core, ty),
+                )
+            )
+        parts[pl.ds(mine, 1), :, columns] = part[pl.ds(xi, 1), :, columns]
+        return copies
+
+    own_cot.wait()
+    for c in cot_copies + act2_c:
+        c.wait_recv()
+    for k in range(nx):
+        part[k, :, 3 * mid :] = dot(cot_all[k], act2_all[...]).astype(BF16)
     reduce_mid(red)
+    part_copies = send_parts(pl.ds(3 * mid, mid))
     for o in range(1, nz):
         if o not in halo:
             pass_on(dconv_all, dconv_z, dconv_c, o)
-    own_cot.wait()
     own_act.wait()
-    for c in cot_copies + act_copies + act2_c + dconv_c:
+    for c in act_copies + dconv_c:
         c.wait_recv()
 
     depth = nz * 2 * rows
@@ -312,23 +368,14 @@
         part[k, :, 2 * mid : 3 * mid] = dot(
             act_all[k, :, shift:], dconv_all[: depth - shift, :]
         ).astype(BF16)
-        part[k, :, 3 * mid :] = dot(cot_all[k], act2_all[...]).astype(BF16)
-    group = nx * m
-    mine = xi * m + dp
-    part_copies = []
-    for o in range(1, group):
-        to = lax.rem(mine + o, group)
-        tx, ty = lax.div(to, m), lax.rem(to, m)
-        part_copies.append(
-            push(part.at[tx], parts.at[mine], (z * inner + tx * 2 + core, ty))
-        )
-    parts[pl.ds(mine, 1)] = part[pl.ds(xi, 1)]
+    part_copies += send_parts(pl.ds(0, 3 * mid))
 
     mean = reduce_end(red)
     grad_ref[...] = (
         cot_ref[...].astype(F32)
-        + gi_ref[...] * (dact1[...] - mean[0:1] - h1[...] * mean[1:2]) * rs1
+        + gi_ref[...].reshape(1, -1) * (dact1[...] - mean[0:1] - h1[...] * mean[1:2]) * rs1
     ).astype(BF16)
+    stores[1].start()
 
     for c in part_copies:
         c.wait_recv()
@@ -337,6 +384,10 @@
         total = total + parts[k].astype(F32)
     convg_ref[...] = total[:block, : 3 * mid]
     projg_ref[...] = total[:block, 3 * mid :]
+    stores[2].start()
+    stores[3].start()
+    for c in stores:
+        c.wait()
 
     for c in pending:
         c.wait_send()
@@ -348,6 +399,17 @@
     @pl.when(has_prev)
     def _():
         down.wait_send()
+
+
+def copy_kernel(count, *refs):
+    sem = refs[-1]
+    copies = [
+        pltpu.make_async_copy(refs[i], refs[count + i], sem.at[i]) for i in range(count)
+    ]
+    for c in copies:
+        c.start()
+    for c in copies:
+        c.wait()
 
 
 def per_device(inputs, cotangent, conv_weight, proj_weight, gain_in, bias_in, gain_mid, bias_mid):
@@ -358,19 +420,29 @@
     )
     rows, nz, nx, padded = plan.rows, plan.nz, plan.nx, plan.padded
     depth = nz * 2 * rows
-    vmem = pl.BlockSpec(memory_space=pltpu.VMEM)
+    hbm = pl.BlockSpec(memory_space=pl.ANY)
+    outs = (
+        jax.ShapeDtypeStruct((rows, width), BF16),
+        jax.ShapeDtypeStruct((rows, width), BF16),
+        jax.ShapeDtypeStruct((plan.block, 3 * mid), F32),
+        jax.ShapeDtypeStruct((plan.block, mid), F32),
+    )
     phases = len(plan.phases)
-    block_out, input_grad, conv_grad, proj_grad = pl.pallas_call(
+    results = pl.pallas_call(
         functools.partial(kernel, plan),
-        out_shape=(
-            jax.ShapeDtypeStruct((rows, width), BF16),
-            jax.ShapeDtypeStruct((rows, width), BF16),
-            jax.ShapeDtypeStruct((plan.block, 3 * mid), F32),
-            jax.ShapeDtypeStruct((plan.block, mid), F32),
-        ),
-        in_specs=[vmem] * 8,
-        out_specs=(vmem,) * 4,
+        out_shape=outs,
+        in_specs=[hbm] * 8,
+        out_specs=(hbm,) * 4,
         scratch_shapes=[
+            pltpu.VMEM((rows, width), BF16),
+            pltpu.VMEM((rows, width), BF16),
+            pltpu.VMEM((width, 3 * mid), BF16),
+            pltpu.VMEM((mid, width), BF16),
+            pltpu.VMEM((width,), F32),
+            pltpu.VMEM((width,), F32),
+            pltpu.VMEM((mid,), F32),
+            pltpu.VMEM((mid,), F32),
+            *[pltpu.VMEM(o.shape, o.dtype) for o in outs],
             pltpu.VMEM((2, phases, 2, width), F32),
             pltpu.VMEM((2, phases, 2, mid), F32),
             pltpu.VMEM((2, plan.slots, 2, width), F32),
@@ -394,21 +466,29 @@
             pltpu.VMEM((nx * plan.m, padded, 4 * mid), BF16),
             pltpu.SemaphoreType.DMA((plan.sems,)),
             pltpu.SemaphoreType.DMA((plan.sems,)),
-            pltpu.SemaphoreType.DMA((2,)),
+            pltpu.SemaphoreType.DMA((14,)),
         ],
         compiler_params=pltpu.CompilerParams(
-            collective_id=0, has_side_effects=True, vmem_limit_bytes=32 * 1024 * 1024
+            collective_id=0, has_side_effects=True, vmem_limit_bytes=56 * 1024 * 1024
         ),
     )(
         inputs.reshape(rows, width),
         cotangent.reshape(rows, width),
         conv_weight,
         proj_weight,
-        gain_in.reshape(1, width),
-        bias_in.reshape(1, width),
-        gain_mid.reshape(1, mid),
-        bias_mid.reshape(1, mid),
+        gain_in,
+        bias_in,
+        gain_mid,
+        bias_mid,
     )
+    block_out, input_grad, conv_grad, proj_grad = pl.pallas_call(
+        functools.partial(copy_kernel, len(outs)),
+        out_shape=outs,
+        in_specs=[hbm] * len(outs),
+        out_specs=(hbm,) * len(outs),
+        scratch_shapes=[pltpu.SemaphoreType.DMA((len(outs),))],
+        compiler_params=pltpu.CompilerParams(vmem_limit_bytes=56 * 1024 * 1024),
+    )(*results)
     shape = (samples, places, width)
     return (block_out.reshape(shape), input_grad.reshape(shape), conv_grad, proj_grad)
 

time: 63.5 us -> 71.9 us (1.13)
  Pallas kernels: 53.1 us -> 71.1 us
  local copies, waits for them, and re-layouts: 9.49 us -> 0 us
    pallas_call x1 -> x2, Pallas kernels: 53.1 us -> 71.1 us  [the longest x1 52.1 us: per_device(): pl.pallas_call(functools.partial(kernel, plan), out_shape=outs, in_specs=...]
    unnamed x16 -> x0, local copies, waits for them, and re-layouts: 8.11 us -> none
    reshape x2 -> x0, local copies, waits for them, and re-layouts: 1.38 us -> none  [the longest x1 0.69 us: per_device(): gain_in.reshape(1, width)]
where the time goes in v2:
time: 71.9 us; the launch traced here: 71.8 us
  Pallas kernels  71.1 us (99%)
    pallas_call x1, Pallas kernels, per_device(): pl.pallas_call(functools.partial(kernel, plan), out_shape=outs, in_specs=...  52.1 us
    pallas_call x1, Pallas kernels, per_device(): pl.pallas_call(functools.partial(copy_kernel, len(outs)), out_shape=outs,...  19 us

profile of v2, /device:TPU:0, one launch (start us, length us, event | category | flops | bytes accessed | tf_op | source)
XLA Modules:
  0.0 71.8 jit_solution(309614216862916793)
XLA Ops:
  0.6 52.1 %shard_map.111 = (bf16[128,768]{1,0:T(8,128)(2,1)}, bf16[128,768]{1,0:T(8,128)(2,1)}, f32[48,768]{1,0:T(8,128)}, f32[48,256]{1,0:T(8,128)}) custom-call(bf16[128,768]{1,0:T(8,128)(2,1)} %bitcast.4, bf16[128,768]{1,0:T(8,128)(2,1)} %bitcast.5, bf16[768,768]{1,0:T(8,128)(2,1)} %cw_hbm.1, bf16[256,768]{1,0:T(8,128)(2,1)} %pw_hbm.1, f32[768]{0:T(1024)} %gi_hbm.1, ...), custom_call_target="tpu_custom_call" | custom-call | tf_op jit(solution)/shard_map/pallas_call | solution.py:431
  52.7 19.0 %shard_map.112 = (bf16[128,768]{1,0:T(8,128)(2,1)}, bf16[128,768]{1,0:T(8,128)(2,1)}, f32[48,768]{1,0:T(8,128)}, f32[48,256]{1,0:T(8,128)}) custom-call(bf16[128,768]{1,0:T(8,128)(2,1)} %get-tuple-element.12.refs_0_, bf16[128,768]{1,0:T(8,128)(2,1)} %get-tuple-element.13.refs_1_, f32[48,768]{1,0:T(8,128)} %get-tuple-element.14.refs_2_, ...), custom_call_target="tpu_custom_call" | custom-call | tf_op jit(solution)/shard_map/pallas_call | solution.py:484

commit v3 on v2

--- a/solution.py
+++ b/solution.py
@@ -73,7 +73,7 @@
     out_ref, grad_ref, convg_ref, projg_ref,
     src_w, src_m, got_w, got_m,
     act, h1, pre1, inner1, dact2, before, after, ysend, dact1,
-    cot_t, act_t, cot_all, act_all, act2_all, dconv_all, part, parts,
+    cot_t, act_t, cot_all, act_all, act2_all, dconv_all, part, parts, acc,
     send_sem, recv_sem, local_sem,
 ):
     n, m, nz, nx, inner = plan.n, plan.m, plan.nz, plan.nx, plan.inner
@@ -349,25 +349,42 @@
         c.wait_recv()
     for k in range(nx):
         part[k, :, 3 * mid :] = dot(cot_all[k], act2_all[...]).astype(BF16)
+    acc[...] = jnp.zeros_like(acc)
+    own_act.wait()
+    for c in act_copies:
+        c.wait_recv()
+
+    def add_plane(o, passed):
+        dconv_c[passed].wait_recv()
+        p = lax.rem(z + nz - o, nz)
+        span = 2 * rows
+        g = dconv_all[pl.ds(pl.multiple_of(p * span, span), span), :]
+
+        def add(tap, q):
+            a = act_all[:, :, pl.ds(pl.multiple_of(q * span, span), span)]
+            acc[:, tap * mid : (tap + 1) * mid] += dot(a.reshape(nx * padded, span), g)
+
+        add(1, p)
+
+        @pl.when(p >= plan.hz)
+        def _():
+            add(0, p - plan.hz)
+
+        @pl.when(p + plan.hz < nz)
+        def _():
+            add(2, p + plan.hz)
+
+    add_plane(0, 0)
+    for i, o in enumerate(halo):
+        add_plane(o, 1 + i)
     reduce_mid(red)
     part_copies = send_parts(pl.ds(3 * mid, mid))
-    for o in range(1, nz):
-        if o not in halo:
-            pass_on(dconv_all, dconv_z, dconv_c, o)
-    own_act.wait()
-    for c in act_copies + dconv_c:
-        c.wait_recv()
-
-    depth = nz * 2 * rows
-    shift = plan.hz * 2 * rows
-    for k in range(nx):
-        part[k, :, :mid] = dot(
-            act_all[k, :, : depth - shift], dconv_all[shift:, :]
-        ).astype(BF16)
-        part[k, :, mid : 2 * mid] = dot(act_all[k], dconv_all[...]).astype(BF16)
-        part[k, :, 2 * mid : 3 * mid] = dot(
-            act_all[k, :, shift:], dconv_all[: depth - shift, :]
-        ).astype(BF16)
+    rest = [o for o in range(1, nz) if o not in halo]
+    for o in rest:
+        pass_on(dconv_all, dconv_z, dconv_c, o)
+    for i, o in enumerate(rest):
+        add_plane(o, 1 + len(halo) + i)
+    part[:, :, : 3 * mid] = acc[...].reshape(nx, padded, 3 * mid).astype(BF16)
     part_copies += send_parts(pl.ds(0, 3 * mid))
 
     mean = reduce_end(red)
@@ -402,14 +419,8 @@
 
 
 def copy_kernel(count, *refs):
-    sem = refs[-1]
-    copies = [
-        pltpu.make_async_copy(refs[i], refs[count + i], sem.at[i]) for i in range(count)
-    ]
-    for c in copies:
-        c.start()
-    for c in copies:
-        c.wait()
+    for i in range(count):
+        refs[count + i][...] = refs[i][...]
 
 
 def per_device(inputs, cotangent, conv_weight, proj_weight, gain_in, bias_in, gain_mid, bias_mid):
@@ -421,6 +432,7 @@
     rows, nz, nx, padded = plan.rows, plan.nz, plan.nx, plan.padded
     depth = nz * 2 * rows
     hbm = pl.BlockSpec(memory_space=pl.ANY)
+    vmem = pl.BlockSpec(memory_space=pltpu.VMEM)
     outs = (
         jax.ShapeDtypeStruct((rows, width), BF16),
         jax.ShapeDtypeStruct((rows, width), BF16),
@@ -464,6 +476,7 @@
             pltpu.VMEM((depth, mid), BF16),
             pltpu.VMEM((nx, padded, 4 * mid), BF16),
             pltpu.VMEM((nx * plan.m, padded, 4 * mid), BF16),
+            pltpu.VMEM((nx * padded, 3 * mid), F32),
             pltpu.SemaphoreType.DMA((plan.sems,)),
             pltpu.SemaphoreType.DMA((plan.sems,)),
             pltpu.SemaphoreType.DMA((14,)),
@@ -484,9 +497,8 @@
     block_out, input_grad, conv_grad, proj_grad = pl.pallas_call(
         functools.partial(copy_kernel, len(outs)),
         out_shape=outs,
-        in_specs=[hbm] * len(outs),
-        out_specs=(hbm,) * len(outs),
-        scratch_shapes=[pltpu.SemaphoreType.DMA((len(outs),))],
+        in_specs=[vmem] * len(outs),
+        out_specs=(vmem,) * len(outs),
         compiler_params=pltpu.CompilerParams(vmem_limit_bytes=56 * 1024 * 1024),
     )(*results)
     shape = (samples, places, width)

time: 71.9 us -> 55.2 us (0.77)
  Pallas kernels: 71.1 us -> 54.4 us
    pallas_call x1, Pallas kernels: 19 us -> 1.92 us  [per_device(): pl.pallas_call(functools.partial(copy_kernel, len(outs)), out_shape=outs,...]
where the time goes in v3:
time: 55.2 us; the launch traced here: 55.1 us
  Pallas kernels  54.4 us (99%)
  between operations  0.64 us (1%)
    pallas_call x1, Pallas kernels, per_device(): pl.pallas_call(functools.partial(kernel, plan), out_shape=outs, in_specs=...  52.5 us
    pallas_call x1, Pallas kernels, per_device(): pl.pallas_call(functools.partial(copy_kernel, len(outs)), out_shape=outs,...  1.92 us

profile of v3, /device:TPU:0, one launch (start us, length us, event | category | flops | bytes accessed | tf_op | source)
XLA Modules:
  0.0 55.1 jit_solution(14822522338426153061)
XLA Ops:
  0.6 52.5 %shard_map.111 = (bf16[128,768]{1,0:T(8,128)(2,1)}, bf16[128,768]{1,0:T(8,128)(2,1)}, f32[48,768]{1,0:T(8,128)}, f32[48,256]{1,0:T(8,128)}) custom-call(bf16[128,768]{1,0:T(8,128)(2,1)} %bitcast.4, bf16[128,768]{1,0:T(8,128)(2,1)} %bitcast.5, bf16[768,768]{1,0:T(8,128)(2,1)} %cw_hbm.1, bf16[256,768]{1,0:T(8,128)(2,1)} %pw_hbm.1, f32[768]{0:T(1024)} %gi_hbm.1, ...), custom_call_target="tpu_custom_call" | custom-call | tf_op jit(solution)/shard_map/pallas_call | solution.py:443
  53.1 1.9 %shard_map.112 = (bf16[128,768]{1,0:T(8,128)(2,1)}, bf16[128,768]{1,0:T(8,128)(2,1)}, f32[48,768]{1,0:T(8,128)}, f32[48,256]{1,0:T(8,128)}) custom-call(bf16[128,768]{1,0:T(8,128)(2,1)} %get-tuple-element.12.refs_0_, bf16[128,768]{1,0:T(8,128)(2,1)} %get-tuple-element.13.refs_1_, f32[48,768]{1,0:T(8,128)} %get-tuple-element.14.refs_2_, ...), custom_call_target="tpu_custom_call" | custom-call | tf_op jit(solution)/shard_map/pallas_call | solution.py:497

commit v4 on v3

--- a/solution.py
+++ b/solution.py
@@ -10,6 +10,7 @@
 
 DILATION = 1024
 EPS = 1e-05
+EXTRA = 16
 COEFF = math.sqrt(2.0 / math.pi)
 MESH = pl.DeviceIdType.MESH
 F32, BF16 = jnp.float32, jnp.bfloat16
@@ -37,6 +38,21 @@
     return jnp.concatenate(
         [jnp.sum(a, axis=0, keepdims=True), jnp.sum(b, axis=0, keepdims=True)], axis=0
     )
+
+
+def packed(v):
+    m = jnp.mean(v, axis=0, keepdims=True)
+    high = m.astype(BF16).astype(F32)
+    mid = (m - high).astype(BF16).astype(F32)
+    low = m - high - mid
+    pad = jnp.zeros((EXTRA - 3, v.shape[1]), F32)
+    return jnp.concatenate([v - m, high, mid, low, pad], axis=0).astype(BF16)
+
+
+def unpacked(v):
+    f = v.astype(F32)
+    r = v.shape[0] - EXTRA
+    return f[:r] + (f[r : r + 1] + f[r + 1 : r + 2] + f[r + 2 : r + 3])
 
 
 class Plan:
@@ -73,7 +89,7 @@
     out_ref, grad_ref, convg_ref, projg_ref,
     src_w, src_m, got_w, got_m,
     act, h1, pre1, inner1, dact2, before, after, ysend, dact1,
-    cot_t, act_t, cot_all, act_all, act2_all, dconv_all, part, parts, acc,
+    cot_t, act_t, cot_all, act_all, act2_all, dconv_all, dact_all, conv_all, part, parts, acc,
     send_sem, recv_sem, local_sem,
 ):
     n, m, nz, nx, inner = plan.n, plan.m, plan.nz, plan.nx, plan.inner
@@ -206,13 +222,32 @@
                 )
         return copies, own
 
+    def place(zz, c, size=rows):
+        return pl.ds(pl.multiple_of((zz * 2 + c) * size, size), size)
+
+    long = rows + EXTRA
+    own = place(z, core)
+    halo = sorted({plan.hz, nz - plan.hz})
+    rest = [o for o in range(1, nz) if o not in halo]
+
+    def gather_start(full, size):
+        at = full.at[place(z, core, size)]
+        over_z = {o: push(at, at, z_peer(o)) for o in halo + rest}
+        return over_z, {0: push(at, at, core_peer)}
+
+    def pass_on(full, size, over_z, across, o):
+        over_z[o].wait_recv()
+        piece = full.at[place(lax.rem(z + nz - o, nz), core, size)]
+        across[o] = push(piece, piece, core_peer)
+
     loads[1].wait()
     loads[2].wait()
-    cot = cot_ref[...]
-    stage_columns(cot.astype(F32), cot_t)
+    dact = dot_t(cot_ref[...], pw_ref[...])
+    dact2[...] = dact
+    dact_all[own, :] = dact.astype(BF16)
     reduce_step(red)
-    cot_copies, own_cot = spread_columns(cot_t, cot_all, local_sem.at[0])
-    dact2[...] = dot_t(cot_ref[...], pw_ref[...])
+    dact_z, dact_c = gather_start(dact_all, rows)
+    stage_columns(cot_ref[...].astype(F32), cot_t)
     for c in loads[3:]:
         c.wait()
 
@@ -234,12 +269,12 @@
 
     @pl.when(has_next)
     def _():
-        ysend[0] = dot(act[...], cw_ref[:, :mid]).astype(BF16)
+        ysend[0] = packed(dot(act[...], cw_ref[:, :mid]))
         up.start()
 
     @pl.when(has_prev)
     def _():
-        ysend[1] = dot(act[...], cw_ref[:, 2 * mid :]).astype(BF16)
+        ysend[1] = packed(dot(act[...], cw_ref[:, 2 * mid :]))
         down.start()
 
     conv = dot(act[...], cw_ref[:, mid : 2 * mid])
@@ -261,11 +296,15 @@
     def _():
         after[...] = jnp.zeros_like(after)
 
-    conv = conv + before[...].astype(F32) + after[...].astype(F32)
+    conv = conv + unpacked(before[...]) + unpacked(after[...])
     src_m[0, 0] = column_sums(conv, conv * conv)
     red = reduce_start(src_m, got_m, 0)
+    conv_all[place(z, core, long), :] = packed(conv)
+    for o in halo + rest:
+        pass_on(dact_all, rows, dact_z, dact_c, o)
+    reduce_step(red)
+    conv_z, conv_c = gather_start(conv_all, long)
     pre1[...] = gelu_slope(pre1[...], inner1[...])
-    reduce_step(red)
     act_copies, own_act = spread_columns(act_t, act_all, local_sem.at[1])
     mean = reduce_end(red)
     center = mean[0:1]
@@ -278,36 +317,33 @@
     src_m[1, 0] = column_sums(dpre2, dpre2 * h2)
     red = reduce_start(src_m, got_m, 1)
 
-    def place(zz, c):
-        return pl.ds(pl.multiple_of((zz * 2 + c) * rows, rows), rows)
-
-    own = place(z, core)
-
-    def gather_start(full):
-        order = sorted(range(1, nz), key=lambda o: o not in (plan.hz, nz - plan.hz))
-        over_z = {o: push(full.at[own], full.at[own], z_peer(o)) for o in order}
-        return over_z, [push(full.at[own], full.at[own], core_peer)]
-
-    def pass_on(full, over_z, across, o):
-        over_z[o].wait_recv()
-        piece = full.at[place(lax.rem(z + nz - o, nz), core)]
-        across.append(push(piece, piece, core_peer))
-
     act2_all[own, :] = act2
-    reduce_step(red)
-    act2_z, act2_c = gather_start(act2_all)
     out_ref[...] = (x_ref[...].astype(F32) + dot(act2, pw_ref[...])).astype(BF16)
     stores[0].start()
-    mean = reduce_end(red)
-    dconv = (gm_ref[...].reshape(1, -1) * (dpre2 - mean[0:1] - h2 * mean[1:2]) * rs2).astype(BF16)
-    dconv_all[own, :] = dconv
-    dconv_z, dconv_c = gather_start(dconv_all)
-    dact1[...] = dot_t(dconv, cw_ref[:, mid : 2 * mid])
-    for o in range(1, nz):
-        pass_on(act2_all, act2_z, act2_c, o)
-    halo = sorted({plan.hz, nz - plan.hz})
+    reduce_step(red)
+    cot_copies, own_cot = spread_columns(cot_t, cot_all, local_sem.at[0])
+    for o in halo + rest:
+        pass_on(conv_all, long, conv_z, conv_c, o)
+
+    def remake(o, c):
+        zz = lax.rem(z + nz - o, nz)
+        h = (unpacked(conv_all[place(zz, c, long), :]) - center) * rs2
+        pre = gm_ref[...].reshape(1, -1) * h + bm_ref[...].reshape(1, -1)
+        t = gelu_inner(pre)
+        act2_all[place(zz, c), :] = (0.5 * pre * (1.0 + t)).astype(BF16)
+        return h, dact_all[place(zz, c), :].astype(F32) * gelu_slope(pre, t)
+
+    def remake_dconv(o, c, h, d):
+        zz = lax.rem(z + nz - o, nz)
+        dconv_all[place(zz, c), :] = (scale2 * (d - mean2[0:1] - h * mean2[1:2])).astype(BF16)
+
+    remade = {o: remake(o, core) for o in halo}
+    mean2 = reduce_end(red)
+    scale2 = gm_ref[...].reshape(1, -1) * rs2
+    remake_dconv(0, core, h2, dpre2)
     for o in halo:
-        pass_on(dconv_all, dconv_z, dconv_c, o)
+        remake_dconv(o, core, *remade[o])
+    dact1[...] = dot_t(dconv_all[own, :], cw_ref[:, mid : 2 * mid])
 
     @pl.when(z + plan.hz < nz)
     def _():
@@ -344,18 +380,12 @@
         parts[pl.ds(mine, 1), :, columns] = part[pl.ds(xi, 1), :, columns]
         return copies
 
-    own_cot.wait()
-    for c in cot_copies + act2_c:
-        c.wait_recv()
-    for k in range(nx):
-        part[k, :, 3 * mid :] = dot(cot_all[k], act2_all[...]).astype(BF16)
     acc[...] = jnp.zeros_like(acc)
     own_act.wait()
     for c in act_copies:
         c.wait_recv()
 
-    def add_plane(o, passed):
-        dconv_c[passed].wait_recv()
+    def add_plane(o):
         p = lax.rem(z + nz - o, nz)
         span = 2 * rows
         g = dconv_all[pl.ds(pl.multiple_of(p * span, span), span), :]
@@ -374,18 +404,22 @@
         def _():
             add(2, p + plan.hz)
 
-    add_plane(0, 0)
-    for i, o in enumerate(halo):
-        add_plane(o, 1 + i)
+    for o in rest:
+        remake_dconv(o, core, *remake(o, core))
+    for o in [0] + halo + rest:
+        dact_c[o].wait_recv()
+        conv_c[o].wait_recv()
+        remake_dconv(o, 1 - core, *remake(o, 1 - core))
+        add_plane(o)
+    part[:, :, : 3 * mid] = acc[...].reshape(nx, padded, 3 * mid).astype(BF16)
     reduce_mid(red)
-    part_copies = send_parts(pl.ds(3 * mid, mid))
-    rest = [o for o in range(1, nz) if o not in halo]
-    for o in rest:
-        pass_on(dconv_all, dconv_z, dconv_c, o)
-    for i, o in enumerate(rest):
-        add_plane(o, 1 + len(halo) + i)
-    part[:, :, : 3 * mid] = acc[...].reshape(nx, padded, 3 * mid).astype(BF16)
-    part_copies += send_parts(pl.ds(0, 3 * mid))
+    part_copies = send_parts(pl.ds(0, 3 * mid))
+    own_cot.wait()
+    for c in cot_copies:
+        c.wait_recv()
+    for k in range(nx):
+        part[k, :, 3 * mid :] = dot(cot_all[k], act2_all[...]).astype(BF16)
+    part_copies += send_parts(pl.ds(3 * mid, mid))
 
     mean = reduce_end(red)
     grad_ref[...] = (
@@ -464,9 +498,9 @@
             pltpu.VMEM((rows, width), F32),
             pltpu.VMEM((rows, width), F32),
             pltpu.VMEM((rows, mid), F32),
-            pltpu.VMEM((rows, mid), BF16),
-            pltpu.VMEM((rows, mid), BF16),
-            pltpu.VMEM((2, rows, mid), BF16),
+            pltpu.VMEM((rows + EXTRA, mid), BF16),
+            pltpu.VMEM((rows + EXTRA, mid), BF16),
+            pltpu.VMEM((2, rows + EXTRA, mid), BF16),
             pltpu.VMEM((rows, width), F32),
             pltpu.VMEM((nz, nx, 2, padded, rows), BF16),
             pltpu.VMEM((nz, nx, 2, padded, rows), BF16),
@@ -474,6 +508,8 @@
             pltpu.VMEM((nx, padded, depth), BF16),
             pltpu.VMEM((depth, mid), BF16),
             pltpu.VMEM((depth, mid), BF16),
+            pltpu.VMEM((depth, mid), BF16),
+            pltpu.VMEM((nz * 2 * (rows + EXTRA), mid), BF16),
             pltpu.VMEM((nx, padded, 4 * mid), BF16),
             pltpu.VMEM((nx * plan.m, padded, 4 * mid), BF16),
             pltpu.VMEM((nx * padded, 3 * mid), F32),

time: 55.2 us -> 52.7 us (0.955)
  Pallas kernels: 54.4 us -> 51.9 us
    pallas_call x1, Pallas kernels: 52.5 us -> 50 us  [per_device(): pl.pallas_call(functools.partial(kernel, plan), out_shape=outs, in_specs=...]
where the time goes in v4:
time: 52.7 us; the launch traced here: 52.5 us
  Pallas kernels  51.9 us (98%)
  between operations  0.64 us (1%)
    pallas_call x1, Pallas kernels, per_device(): pl.pallas_call(functools.partial(kernel, plan), out_shape=outs, in_specs=...  50 us
    pallas_call x1, Pallas kernels, per_device(): pl.pallas_call(functools.partial(copy_kernel, len(outs)), out_shape=outs,...  1.92 us

profile of v4, /device:TPU:0, one launch (start us, length us, event | category | flops | bytes accessed | tf_op | source)
XLA Modules:
  0.0 52.5 jit_solution(3053159132213694737)
XLA Ops:
  0.6 50.0 %shard_map.111 = (bf16[128,768]{1,0:T(8,128)(2,1)}, bf16[128,768]{1,0:T(8,128)(2,1)}, f32[48,768]{1,0:T(8,128)}, f32[48,256]{1,0:T(8,128)}) custom-call(bf16[128,768]{1,0:T(8,128)(2,1)} %bitcast.4, bf16[128,768]{1,0:T(8,128)(2,1)} %bitcast.5, bf16[768,768]{1,0:T(8,128)(2,1)} %cw_hbm.1, bf16[256,768]{1,0:T(8,128)(2,1)} %pw_hbm.1, f32[768]{0:T(1024)} %gi_hbm.1, ...), custom_call_target="tpu_custom_call" | custom-call | tf_op jit(solution)/shard_map/pallas_call | solution.py:477
  50.6 1.9 %shard_map.112 = (bf16[128,768]{1,0:T(8,128)(2,1)}, bf16[128,768]{1,0:T(8,128)(2,1)}, f32[48,768]{1,0:T(8,128)}, f32[48,256]{1,0:T(8,128)}) custom-call(bf16[128,768]{1,0:T(8,128)(2,1)} %get-tuple-element.12.refs_0_, bf16[128,768]{1,0:T(8,128)(2,1)} %get-tuple-element.13.refs_1_, f32[48,768]{1,0:T(8,128)} %get-tuple-element.14.refs_2_, ...), custom_call_target="tpu_custom_call" | custom-call | tf_op jit(solution)/shard_map/pallas_call | solution.py:533

commit v5 on v4

--- a/solution.py
+++ b/solution.py
@@ -53,6 +53,22 @@
     f = v.astype(F32)
     r = v.shape[0] - EXTRA
     return f[:r] + (f[r : r + 1] + f[r + 1 : r + 2] + f[r + 2 : r + 3])
+
+
+def fold(v):
+    return jnp.sum(v.reshape(v.shape[0] // 8, 8, v.shape[1]), axis=0)
+
+
+def each(count, size, body):
+    def step(i, carry):
+        new = body(pl.ds(pl.multiple_of(i * size, size), size), i * size)
+        return tuple(a + fold(b) for a, b in zip(carry, new or ()))
+
+    def run(width=None):
+        init = () if width is None else (jnp.zeros((8, width), F32),) * 2
+        return lax.fori_loop(0, count // size, step, init)
+
+    return run
 
 
 class Plan:
@@ -70,11 +86,11 @@
         assert 0 < self.hz < self.nz
         self.block = width // n
         self.padded = -(-self.block // 16) * 16
-        if inner * m <= 8:
-            self.phases = ("z", "plane")
+        if n * m <= 32:
+            self.phases = ("core", "chips")
         else:
             self.phases = ("z", "lo", "dp")
-        size = {"plane": inner * m, "lo": inner, "dp": m, "z": self.nz}
+        size = {"core": 2, "chips": n * m // 2, "lo": inner, "dp": m, "z": self.nz}
         self.sizes = [size[p] for p in self.phases]
         self.slots = sum(s - 1 for s in self.sizes)
         q = self.nz * 2 - 1
@@ -88,8 +104,8 @@
     x_ref, cot_ref, cw_ref, pw_ref, gi_ref, bi_ref, gm_ref, bm_ref,
     out_ref, grad_ref, convg_ref, projg_ref,
     src_w, src_m, got_w, got_m,
-    act, h1, pre1, inner1, dact2, before, after, ysend, dact1,
-    cot_t, act_t, cot_all, act_all, act2_all, dconv_all, dact_all, conv_all, part, parts, acc,
+    act, h1, slope1, mids, dact2, before, after, ysend, dact1,
+    cot_t, act_t, cot_all, act_all, act2_all, dconv_all, dact_all, conv_all, part, parts, acc, stacked, kept,
     send_sem, recv_sem, local_sem,
 ):
     n, m, nz, nx, inner = plan.n, plan.m, plan.nz, plan.nx, plan.inner
@@ -142,8 +158,13 @@
         c = core if c is None else c
         return (lax.rem(z + o, nz) * inner + xi * 2 + c, dp)
 
+    def chip_peer(o):
+        j = lax.rem((z * nx + xi) * m + dp + o, n * m // 2)
+        return (lax.div(j, m) * 2 + core, lax.rem(j, m))
+
     peers = {
-        "plane": plane_peer,
+        "core": lambda o: core_peer,
+        "chips": chip_peer,
         "lo": lambda o: (z * inner + lax.rem(lo + o, inner), dp),
         "dp": lambda o: (me, lax.rem(dp + o, m)),
         "z": z_peer,
@@ -188,13 +209,21 @@
 
     barrier = pltpu.get_barrier_semaphore()
     friends = [plane_peer(o) for o in range(1, inner * m)]
-    friends += [z_peer(o, c) for o in range(1, nz) for c in (core, 1 - core)]
+    if "chips" in plan.phases:
+        friends = [chip_peer(o) for o in range(1, n * m // 2)] + [core_peer]
+        friends += [z_peer(o, 1 - core) for o in range(1, nz)]
+    else:
+        friends += [z_peer(o, c) for o in range(1, nz) for c in (core, 1 - core)]
     for f in friends:
         pl.semaphore_signal(barrier, inc=1, device_id=f, device_id_type=MESH)
 
     loads[0].wait()
-    x = x_ref[...].astype(F32)
-    src_w[0, 0] = column_sums(x, x * x)
+
+    def input_sums(at, _):
+        v = x_ref[at, :].astype(F32)
+        return v, v * v
+
+    src_w[0, 0] = column_sums(*each(rows, 32, input_sums)(width))
     pl.semaphore_wait(barrier, len(friends))
     red = reduce_start(src_w, got_w, 0)
 
@@ -246,21 +275,25 @@
     dact2[...] = dact
     dact_all[own, :] = dact.astype(BF16)
     reduce_step(red)
+    stage_columns(cot_ref[...].astype(F32), cot_t)
     dact_z, dact_c = gather_start(dact_all, rows)
-    stage_columns(cot_ref[...].astype(F32), cot_t)
     for c in loads[3:]:
         c.wait()
 
     mean = reduce_end(red)
     center = mean[0:1]
     rs1 = 1.0 / jnp.sqrt(mean[1:2] - center * center + EPS)
-    h = (x_ref[...].astype(F32) - center) * rs1
-    h1[...] = h
-    pre = gi_ref[...].reshape(1, -1) * h + bi_ref[...].reshape(1, -1)
-    t = gelu_inner(pre)
-    pre1[...] = pre
-    inner1[...] = t
-    act[...] = (0.5 * pre * (1.0 + t)).astype(BF16)
+    gain_in, bias_in = gi_ref[...].reshape(1, -1), bi_ref[...].reshape(1, -1)
+
+    def first_gelu(at, _):
+        h = (x_ref[at, :].astype(F32) - center) * rs1
+        pre = gain_in * h + bias_in
+        t = gelu_inner(pre)
+        act[at, :] = (0.5 * pre * (1.0 + t)).astype(BF16)
+        h1[at, :] = h
+        slope1[at, :] = gelu_slope(pre, t)
+
+    each(rows, 16, first_gelu)()
 
     steps = plan.hz * inner
     up = copy_to(ysend.at[0], before, (lax.rem(me + steps, n), dp))
@@ -277,7 +310,8 @@
         ysend[1] = packed(dot(act[...], cw_ref[:, 2 * mid :]))
         down.start()
 
-    conv = dot(act[...], cw_ref[:, mid : 2 * mid])
+    conv, h2, dpre2 = (mids.at[:, k * mid : (k + 1) * mid] for k in range(3))
+    conv[...] = dot(act[...], cw_ref[:, mid : 2 * mid])
     stage_columns(act[...].astype(F32), act_t)
 
     @pl.when(has_prev)
@@ -296,70 +330,119 @@
     def _():
         after[...] = jnp.zeros_like(after)
 
-    conv = conv + unpacked(before[...]) + unpacked(after[...])
-    src_m[0, 0] = column_sums(conv, conv * conv)
+    def mean_row(ref, start):
+        tail = ref[pl.ds(start, EXTRA), :].astype(F32)
+        return tail[0:1] + tail[1:2] + tail[2:3]
+
+    mean_halo = mean_row(before, rows) + mean_row(after, rows)
+
+    def conv_sums(at, _):
+        v = conv[at, :] + before[at, :].astype(F32) + after[at, :].astype(F32) + mean_halo
+        conv[at, :] = v
+        return v, v * v
+
+    src_m[0, 0] = column_sums(*each(rows, 32, conv_sums)(mid))
     red = reduce_start(src_m, got_m, 0)
-    conv_all[place(z, core, long), :] = packed(conv)
+    conv_all[place(z, core, long), :] = packed(conv[...])
+    reduce_step(red)
     for o in halo + rest:
         pass_on(dact_all, rows, dact_z, dact_c, o)
-    reduce_step(red)
     conv_z, conv_c = gather_start(conv_all, long)
-    pre1[...] = gelu_slope(pre1[...], inner1[...])
     act_copies, own_act = spread_columns(act_t, act_all, local_sem.at[1])
     mean = reduce_end(red)
     center = mean[0:1]
     rs2 = 1.0 / jnp.sqrt(mean[1:2] - center * center + EPS)
-    h2 = (conv - center) * rs2
-    pre2 = gm_ref[...].reshape(1, -1) * h2 + bm_ref[...].reshape(1, -1)
-    t2 = gelu_inner(pre2)
-    act2 = (0.5 * pre2 * (1.0 + t2)).astype(BF16)
-    dpre2 = dact2[...] * gelu_slope(pre2, t2)
-    src_m[1, 0] = column_sums(dpre2, dpre2 * h2)
+    gain_mid, bias_mid = gm_ref[...].reshape(1, -1), bm_ref[...].reshape(1, -1)
+
+    def mid_gelu(value):
+        h = (value - center) * rs2
+        pre = gain_mid * h + bias_mid
+        t = gelu_inner(pre)
+        return h, (0.5 * pre * (1.0 + t)).astype(BF16), gelu_slope(pre, t)
+
+    def own_gelu(at, i):
+        h, a, slope = mid_gelu(conv[at, :])
+        d = dact2[at, :] * slope
+        act2_all[pl.ds(pl.multiple_of((z * 2 + core) * rows + i, 32), 32), :] = a
+        h2[at, :] = h
+        dpre2[at, :] = d
+        return d, d * h
+
+    src_m[1, 0] = column_sums(*each(rows, 32, own_gelu)(mid))
     red = reduce_start(src_m, got_m, 1)
 
-    act2_all[own, :] = act2
-    out_ref[...] = (x_ref[...].astype(F32) + dot(act2, pw_ref[...])).astype(BF16)
+    reduce_step(red)
+    out_ref[...] = (x_ref[...].astype(F32) + dot(act2_all[own, :], pw_ref[...])).astype(BF16)
     stores[0].start()
-    reduce_step(red)
     cot_copies, own_cot = spread_columns(cot_t, cot_all, local_sem.at[0])
     for o in halo + rest:
         pass_on(conv_all, long, conv_z, conv_c, o)
 
-    def remake(o, c):
-        zz = lax.rem(z + nz - o, nz)
-        h = (unpacked(conv_all[place(zz, c, long), :]) - center) * rs2
-        pre = gm_ref[...].reshape(1, -1) * h + bm_ref[...].reshape(1, -1)
-        t = gelu_inner(pre)
-        act2_all[place(zz, c), :] = (0.5 * pre * (1.0 + t)).astype(BF16)
-        return h, dact_all[place(zz, c), :].astype(F32) * gelu_slope(pre, t)
-
-    def remake_dconv(o, c, h, d):
-        zz = lax.rem(z + nz - o, nz)
-        dconv_all[place(zz, c), :] = (scale2 * (d - mean2[0:1] - h * mean2[1:2])).astype(BF16)
-
-    remade = {o: remake(o, core) for o in halo}
+    def remake(o, c, use):
+        piece = lax.rem(z + nz - o, nz) * 2 + c
+        offset = mean_row(conv_all, pl.multiple_of(piece * long + rows, 16))
+
+        def body(_, i):
+            there = pl.ds(pl.multiple_of(piece * rows + i, 32), 32)
+            source = pl.ds(pl.multiple_of(piece * long + i, 16), 32)
+            h, a, slope = mid_gelu(conv_all[source, :].astype(F32) + offset)
+            act2_all[there, :] = a
+            use(there, i, h, dact_all[there, :].astype(F32) * slope)
+
+        each(rows, 32, body)()
+
+    def keep(k):
+        def use(_, i, h, d):
+            at = pl.ds(pl.multiple_of(k * rows + i, 32), 32)
+            kept[0, at, :] = h
+            kept[1, at, :] = d
+
+        return use
+
+    for k, o in enumerate(halo):
+        remake(o, core, keep(k))
     mean2 = reduce_end(red)
-    scale2 = gm_ref[...].reshape(1, -1) * rs2
-    remake_dconv(0, core, h2, dpre2)
-    for o in halo:
-        remake_dconv(o, core, *remade[o])
-    dact1[...] = dot_t(dconv_all[own, :], cw_ref[:, mid : 2 * mid])
-
-    @pl.when(z + plan.hz < nz)
-    def _():
-        dact1[...] += dot_t(
-            dconv_all[place(lax.rem(z + plan.hz, nz), core), :], cw_ref[:, :mid]
-        )
-
-    @pl.when(z >= plan.hz)
-    def _():
-        dact1[...] += dot_t(
-            dconv_all[place(lax.rem(z + nz - plan.hz, nz), core), :], cw_ref[:, 2 * mid :]
-        )
-
-    dpre1 = dact1[...] * pre1[...]
-    dact1[...] = dpre1
-    src_w[1, 0] = column_sums(dpre1, dpre1 * h1[...])
+    scale2, first2, second2 = gain_mid * rs2, mean2[0:1], mean2[1:2]
+
+    def to_dconv(there, _, h, d):
+        dconv_all[there, :] = (scale2 * (d - first2 - h * second2)).astype(BF16)
+
+    def own_dconv(at, i):
+        v = (scale2 * (dpre2[at, :] - first2 - h2[at, :] * second2)).astype(BF16)
+        dconv_all[pl.ds(pl.multiple_of((z * 2 + core) * rows + i, 32), 32), :] = v
+        stacked[at, mid : 2 * mid] = v
+
+    each(rows, 32, own_dconv)()
+    for k, o in enumerate(halo):
+        piece = lax.rem(z + nz - o, nz) * 2 + core
+
+        def halo_dconv(_, i):
+            at = pl.ds(pl.multiple_of(k * rows + i, 32), 32)
+            there = pl.ds(pl.multiple_of(piece * rows + i, 32), 32)
+            to_dconv(there, i, kept[0, at, :], kept[1, at, :])
+
+        each(rows, 32, halo_dconv)()
+    for has, plane, columns in (
+        (z + plan.hz < nz, z + plan.hz, slice(0, mid)),
+        (z >= plan.hz, z + nz - plan.hz, slice(2 * mid, 3 * mid)),
+    ):
+
+        @pl.when(has)
+        def _():
+            stacked[:, columns] = dconv_all[place(lax.rem(plane, nz), core), :]
+
+        @pl.when(jnp.logical_not(has))
+        def _():
+            stacked[:, columns] = jnp.zeros((rows, mid), BF16)
+
+    dact1[...] = dot_t(stacked[...], cw_ref[...])
+
+    def first_back(at, _):
+        d = dact1[at, :] * slope1[at, :]
+        dact1[at, :] = d
+        return d, d * h1[at, :]
+
+    src_w[1, 0] = column_sums(*each(rows, 16, first_back)(width))
     red = reduce_start(src_w, got_w, 1)
 
     group = nx * m
@@ -404,12 +487,13 @@
         def _():
             add(2, p + plan.hz)
 
+    reduce_step(red)
     for o in rest:
-        remake_dconv(o, core, *remake(o, core))
+        remake(o, core, to_dconv)
     for o in [0] + halo + rest:
         dact_c[o].wait_recv()
         conv_c[o].wait_recv()
-        remake_dconv(o, 1 - core, *remake(o, 1 - core))
+        remake(o, 1 - core, to_dconv)
         add_plane(o)
     part[:, :, : 3 * mid] = acc[...].reshape(nx, padded, 3 * mid).astype(BF16)
     reduce_mid(red)
@@ -422,10 +506,15 @@
     part_copies += send_parts(pl.ds(3 * mid, mid))
 
     mean = reduce_end(red)
-    grad_ref[...] = (
-        cot_ref[...].astype(F32)
-        + gi_ref[...].reshape(1, -1) * (dact1[...] - mean[0:1] - h1[...] * mean[1:2]) * rs1
-    ).astype(BF16)
+    scale1 = gain_in * rs1
+
+    def last(at, _):
+        grad_ref[at, :] = (
+            cot_ref[at, :].astype(F32)
+            + scale1 * (dact1[at, :] - mean[0:1] - h1[at, :] * mean[1:2])
+        ).astype(BF16)
+
+    each(rows, 16, last)()
     stores[1].start()
 
     for c in part_copies:
@@ -513,6 +602,8 @@
             pltpu.VMEM((nx, padded, 4 * mid), BF16),
             pltpu.VMEM((nx * plan.m, padded, 4 * mid), BF16),
             pltpu.VMEM((nx * padded, 3 * mid), F32),
+            pltpu.VMEM((rows, 3 * mid), BF16),
+            pltpu.VMEM((2, 2 * rows, mid), F32),
             pltpu.SemaphoreType.DMA((plan.sems,)),
             pltpu.SemaphoreType.DMA((plan.sems,)),
             pltpu.SemaphoreType.DMA((14,)),

time: 52.7 us -> 50 us (0.949)
  Pallas kernels: 51.9 us -> 49.2 us
    pallas_call x1, Pallas kernels: 50 us -> 47.3 us  [per_device(): pl.pallas_call(functools.partial(kernel, plan), out_shape=outs, in_specs=...]
where the time goes in v5:
time: 50 us; the launch traced here: 49.9 us
  Pallas kernels  49.2 us (98%)
  between operations  0.64 us (1%)
    pallas_call x1, Pallas kernels, per_device(): pl.pallas_call(functools.partial(kernel, plan), out_shape=outs, in_specs=...  47.3 us
    pallas_call x1, Pallas kernels, per_device(): pl.pallas_call(functools.partial(copy_kernel, len(outs)), out_shape=outs,...  1.92 us

profile of v5, /device:TPU:0, one launch (start us, length us, event | category | flops | bytes accessed | tf_op | source)
XLA Modules:
  0.0 49.9 jit_solution(1060310814446516932)
XLA Ops:
  0.6 47.3 %shard_map.111 = (bf16[128,768]{1,0:T(8,128)(2,1)}, bf16[128,768]{1,0:T(8,128)(2,1)}, f32[48,768]{1,0:T(8,128)}, f32[48,256]{1,0:T(8,128)}) custom-call(bf16[128,768]{1,0:T(8,128)(2,1)} %bitcast.4, bf16[128,768]{1,0:T(8,128)(2,1)} %bitcast.5, bf16[768,768]{1,0:T(8,128)(2,1)} %cw_hbm.1, bf16[256,768]{1,0:T(8,128)(2,1)} %pw_hbm.1, f32[768]{0:T(1024)} %gi_hbm.1, ...), custom_call_target="tpu_custom_call" | custom-call | tf_op jit(solution)/shard_map/pallas_call | solution.py:566
  48.0 1.9 %shard_map.112 = (bf16[128,768]{1,0:T(8,128)(2,1)}, bf16[128,768]{1,0:T(8,128)(2,1)}, f32[48,768]{1,0:T(8,128)}, f32[48,256]{1,0:T(8,128)}) custom-call(bf16[128,768]{1,0:T(8,128)(2,1)} %get-tuple-element.12.refs_0_, bf16[128,768]{1,0:T(8,128)(2,1)} %get-tuple-element.13.refs_1_, f32[48,768]{1,0:T(8,128)} %get-tuple-element.14.refs_2_, ...), custom_call_target="tpu_custom_call" | custom-call | tf_op jit(solution)/shard_map/pallas_call | solution.py:624

commit v6 on v5

--- a/solution.py
+++ b/solution.py
@@ -259,14 +259,31 @@
     halo = sorted({plan.hz, nz - plan.hz})
     rest = [o for o in range(1, nz) if o not in halo]
 
+    relay = nz == 4 and plan.hz == 2
+    beside = z + 1 - 2 * lax.rem(z, 2)
+
+    def plane_of(o):
+        if relay and o in (1, 3):
+            return lax.rem(beside + o - 1, nz)
+        return lax.rem(z + nz - o, nz)
+
+    def to_beside(full, size, plane):
+        at = full.at[place(plane, core, size)]
+        return push(at, at, (beside * inner + xi * 2 + core, dp))
+
     def gather_start(full, size):
         at = full.at[place(z, core, size)]
-        over_z = {o: push(at, at, z_peer(o)) for o in halo + rest}
+        if relay:
+            over_z = {2: push(at, at, z_peer(2)), 1: to_beside(full, size, z)}
+        else:
+            over_z = {o: push(at, at, z_peer(o)) for o in halo + rest}
         return over_z, {0: push(at, at, core_peer)}
 
     def pass_on(full, size, over_z, across, o):
         over_z[o].wait_recv()
-        piece = full.at[place(lax.rem(z + nz - o, nz), core, size)]
+        if relay and o == 2:
+            over_z[3] = to_beside(full, size, plane_of(2))
+        piece = full.at[place(plane_of(o), core, size)]
         across[o] = push(piece, piece, core_peer)
 
     loads[1].wait()
@@ -345,7 +362,7 @@
     red = reduce_start(src_m, got_m, 0)
     conv_all[place(z, core, long), :] = packed(conv[...])
     reduce_step(red)
-    for o in halo + rest:
+    for o in halo + rest[:-1]:
         pass_on(dact_all, rows, dact_z, dact_c, o)
     conv_z, conv_c = gather_start(conv_all, long)
     act_copies, own_act = spread_columns(act_t, act_all, local_sem.at[1])
@@ -376,10 +393,11 @@
     stores[0].start()
     cot_copies, own_cot = spread_columns(cot_t, cot_all, local_sem.at[0])
     for o in halo + rest:
-        pass_on(conv_all, long, conv_z, conv_c, o)
+        if o != rest[-1]:
+            pass_on(conv_all, long, conv_z, conv_c, o)
 
     def remake(o, c, use):
-        piece = lax.rem(z + nz - o, nz) * 2 + c
+        piece = plane_of(o) * 2 + c
         offset = mean_row(conv_all, pl.multiple_of(piece * long + rows, 16))
 
         def body(_, i):
@@ -414,7 +432,7 @@
 
     each(rows, 32, own_dconv)()
     for k, o in enumerate(halo):
-        piece = lax.rem(z + nz - o, nz) * 2 + core
+        piece = plane_of(o) * 2 + core
 
         def halo_dconv(_, i):
             at = pl.ds(pl.multiple_of(k * rows + i, 32), 32)
@@ -469,7 +487,7 @@
         c.wait_recv()
 
     def add_plane(o):
-        p = lax.rem(z + nz - o, nz)
+        p = plane_of(o)
         span = 2 * rows
         g = dconv_all[pl.ds(pl.multiple_of(p * span, span), span), :]
 
@@ -488,6 +506,8 @@
             add(2, p + plan.hz)
 
     reduce_step(red)
+    pass_on(dact_all, rows, dact_z, dact_c, rest[-1])
+    pass_on(conv_all, long, conv_z, conv_c, rest[-1])
     for o in rest:
         remake(o, core, to_dconv)
     for o in [0] + halo + rest:

time: 50 us -> 48.3 us (0.966)
  Pallas kernels: 49.2 us -> 47.5 us
    pallas_call x1, Pallas kernels: 47.3 us -> 45.6 us  [per_device(): pl.pallas_call(functools.partial(kernel, plan), out_shape=outs, in_specs=...]
where the time goes in v6:
time: 48.3 us; the launch traced here: 48.1 us
  Pallas kernels  47.5 us (98%)
  between operations  0.64 us (1%)
    pallas_call x1, Pallas kernels, per_device(): pl.pallas_call(functools.partial(kernel, plan), out_shape=outs, in_specs=...  45.6 us
    pallas_call x1, Pallas kernels, per_device(): pl.pallas_call(functools.partial(copy_kernel, len(outs)), out_shape=outs,...  1.92 us

profile of v6, /device:TPU:0, one launch (start us, length us, event | category | flops | bytes accessed | tf_op | source)
XLA Modules:
  0.0 48.1 jit_solution(6117947424370116829)
XLA Ops:
  0.6 45.6 %shard_map.111 = (bf16[128,768]{1,0:T(8,128)(2,1)}, bf16[128,768]{1,0:T(8,128)(2,1)}, f32[48,768]{1,0:T(8,128)}, f32[48,256]{1,0:T(8,128)}) custom-call(bf16[128,768]{1,0:T(8,128)(2,1)} %bitcast.4, bf16[128,768]{1,0:T(8,128)(2,1)} %bitcast.5, bf16[768,768]{1,0:T(8,128)(2,1)} %cw_hbm.1, bf16[256,768]{1,0:T(8,128)(2,1)} %pw_hbm.1, f32[768]{0:T(1024)} %gi_hbm.1, ...), custom_call_target="tpu_custom_call" | custom-call | tf_op jit(solution)/shard_map/pallas_call | solution.py:586
  46.2 1.9 %shard_map.112 = (bf16[128,768]{1,0:T(8,128)(2,1)}, bf16[128,768]{1,0:T(8,128)(2,1)}, f32[48,768]{1,0:T(8,128)}, f32[48,256]{1,0:T(8,128)}) custom-call(bf16[128,768]{1,0:T(8,128)(2,1)} %get-tuple-element.12.refs_0_, bf16[128,768]{1,0:T(8,128)(2,1)} %get-tuple-element.13.refs_1_, f32[48,768]{1,0:T(8,128)} %get-tuple-element.14.refs_2_, ...), custom_call_target="tpu_custom_call" | custom-call | tf_op jit(solution)/shard_map/pallas_call | solution.py:644

commit v7 on v6

--- a/solution.py
+++ b/solution.py
@@ -391,7 +391,6 @@
     reduce_step(red)
     out_ref[...] = (x_ref[...].astype(F32) + dot(act2_all[own, :], pw_ref[...])).astype(BF16)
     stores[0].start()
-    cot_copies, own_cot = spread_columns(cot_t, cot_all, local_sem.at[0])
     for o in halo + rest:
         if o != rest[-1]:
             pass_on(conv_all, long, conv_z, conv_c, o)
@@ -417,6 +416,7 @@
 
         return use
 
+    cot_copies, own_cot = spread_columns(cot_t, cot_all, local_sem.at[0])
     for k, o in enumerate(halo):
         remake(o, core, keep(k))
     mean2 = reduce_end(red)

time: 48.3 us -> 47.6 us (0.986)
  Pallas kernels: 47.5 us -> 46.8 us
    pallas_call x1, Pallas kernels: 45.6 us -> 44.9 us  [per_device(): pl.pallas_call(functools.partial(kernel, plan), out_shape=outs, in_specs=...]
where the time goes in v7:
time: 47.6 us; the launch traced here: 47.5 us
  Pallas kernels  46.8 us (98%)
  between operations  0.64 us (1%)
    pallas_call x1, Pallas kernels, per_device(): pl.pallas_call(functools.partial(kernel, plan), out_shape=outs, in_specs=...  44.9 us
    pallas_call x1, Pallas kernels, per_device(): pl.pallas_call(functools.partial(copy_kernel, len(outs)), out_shape=outs,...  1.92 us

profile of v7, /device:TPU:0, one launch (start us, length us, event | category | flops | bytes accessed | tf_op | source)
XLA Modules:
  0.0 47.5 jit_solution(15359614716409580616)
XLA Ops:
  0.6 44.9 %shard_map.111 = (bf16[128,768]{1,0:T(8,128)(2,1)}, bf16[128,768]{1,0:T(8,128)(2,1)}, f32[48,768]{1,0:T(8,128)}, f32[48,256]{1,0:T(8,128)}) custom-call(bf16[128,768]{1,0:T(8,128)(2,1)} %bitcast.4, bf16[128,768]{1,0:T(8,128)(2,1)} %bitcast.5, bf16[768,768]{1,0:T(8,128)(2,1)} %cw_hbm.1, bf16[256,768]{1,0:T(8,128)(2,1)} %pw_hbm.1, f32[768]{0:T(1024)} %gi_hbm.1, ...), custom_call_target="tpu_custom_call" | custom-call | tf_op jit(solution)/shard_map/pallas_call | solution.py:586
  45.5 1.9 %shard_map.112 = (bf16[128,768]{1,0:T(8,128)(2,1)}, bf16[128,768]{1,0:T(8,128)(2,1)}, f32[48,768]{1,0:T(8,128)}, f32[48,256]{1,0:T(8,128)}) custom-call(bf16[128,768]{1,0:T(8,128)(2,1)} %get-tuple-element.12.refs_0_, bf16[128,768]{1,0:T(8,128)(2,1)} %get-tuple-element.13.refs_1_, f32[48,768]{1,0:T(8,128)} %get-tuple-element.14.refs_2_, ...), custom_call_target="tpu_custom_call" | custom-call | tf_op jit(solution)/shard_map/pallas_call | solution.py:644
